TPU v7x, 128 devices: a whole 4x4x4 slice. The times are simulated.
128 devices in a mesh: sec: 2 (over core), tx: 8 (over y, z_lo), ty: 8 (over z_hi, x).
Axes of the slice: x: 4, y: 4, z: 4 (z_hi: 2, z_lo: 2; z = z_hi * 2 + z_lo), core: 2. Of those that a mesh axis runs over, the one named last changes fastest.
Arguments:
- state: float32 [2, 72, 512, 2048], P('sec', None, 'tx', 'ty'), may hold values from -6 to 6
- coeffs: float32 [2, 3, 512, 2048], P('sec', None, 'tx', 'ty'), may hold values from 0.03 to 0.12
- forcing: float32 [4, 512, 2048], P(None, 'tx', 'ty'), may hold values from -4 to 3, as said below
- levels: int32 [512, 2048], P('tx', 'ty'), may hold values from 0 to 60, as said below
- remap: int32 [5, 2359296], P(None, ('tx', 'ty')), may hold values from 0 to 16383, as said below
Outputs:
- new_state: float32 [2, 72, 512, 2048], P('sec', None, 'tx', 'ty')
- surface_flux: float32 [2, 4, 512, 2048], P('sec', None, 'tx', 'ty')
Inputs may be any that keep to these rules, and one draw needn't show every extreme that they name: `levels`: 0 marks land; 60 is reached. `remap`: each source tile's 36864 links go to nine tiles: tile row -1, 0 or + 4 and tile column -1, 0 or +1 from its own, cyclically; the links come in nine blocks of 4096, one per target tile in the order row step (-1, 0, +4) then column step (-1, 0, +1), and within a block in slot order 0 .. 4095; links of weight 0 carry nothing; weights are 0 to 4; every source tile fills all 4096 slots with nonzero weight toward at least one target tile. `forcing`: winds and precipitation within 3 in size; the previous sea surface temperature lies between -4 and -1.
All inputs are finite; a program needn't handle non-finite values.
Results may differ from a plain program's by a relative error of at most 0.000057.
Values sent between devices are 32-bit elements; how exact they have to be, the bound alone decides.
A program may use at most 128 MiB of HBM per device.

v0:
```python
import functools

import jax
import jax.numpy as jnp
from jax import lax
from jax.sharding import Mesh
from jax.sharding import PartitionSpec as P

CAP = 4096
ASTEPS = 3
OSTEPS = 2
TX_TY = ("tx_0", "tx_1", "ty_0", "ty_1")
TX = ("tx_0", "tx_1")
TY = ("ty_0", "ty_1")
SEC_TX_TY = ("sec", "tx_0", "tx_1", "ty_0", "ty_1")


def extended(cells, sides, width):
    for axis, dim in sides:
        count = lax.axis_size(axis)
        head = lax.slice_in_dim(cells, 0, width, axis=dim)
        tail = lax.slice_in_dim(cells, cells.shape[dim] - width, cells.shape[dim], axis=dim)
        cells = jnp.concatenate(
            [
                lax.ppermute(tail, axis, [(i, (i + 1) % count) for i in range(count)]),
                cells,
                lax.ppermute(head, axis, [((i + 1) % count, i) for i in range(count)]),
            ],
            axis=dim,
        )
    return cells


def extended_2(array, sides, width):
    edges = {}
    for axis, dim in sides:
        size, length = (lax.axis_size(axis), array.shape[dim])
        up = [(i, (i + 1) % size) for i in range(size)]
        last = lax.slice_in_dim(array, length - width, length, axis=dim)
        first = lax.slice_in_dim(array, 0, width, axis=dim)
        edges[dim] = (
            lax.ppermute(last, axis, up),
            lax.ppermute(first, axis, [(b, a) for a, b in up]),
        )
    done = []
    for _, dim in sides:
        low, high = edges[dim]
        around = [(width, width) if d in done else (0, 0) for d in range(array.ndim)]
        array = jnp.concatenate([jnp.pad(low, around), array, jnp.pad(high, around)], axis=dim)
        done.append(dim)
    return array


def passed_along(array, axis, by):
    size = lax.axis_size(axis)
    return lax.ppermute(array, axis, [(i, (i + by) % size) for i in range(size)])


def shifted(value, axis, steps):
    count = lax.axis_size(axis)
    first, last = (max(0, -steps), min(count, count - steps))
    return lax.ppermute(value, axis, [(source, source + steps) for source in range(first, last)])


def over_axes(array, axes):
    return functools.reduce(lax.psum, axes, array)


def neighbours(block):
    return (
        block[..., 2:, 1:-1],
        block[..., :-2, 1:-1],
        block[..., 1:-1, 2:],
        block[..., 1:-1, :-2],
    )


def advance(field, wet, column, mixing, stress):
    level_index = jnp.arange(field.shape[0], dtype=jnp.float32)[:, None, None]
    padded = extended(field, ((TX, 1), (TY, 2)), 1)
    kappa = column[0, 1:-1, 1:-1]
    horiz = jnp.zeros_like(field)
    nears = neighbours(padded)
    for near, near_kap, near_dep in zip(nears, neighbours(column[0]), neighbours(column[1])):
        near_wet = (level_index < near_dep).astype(jnp.float32)
        horiz = horiz + 0.5 * (kappa + near_kap) * wet * near_wet * (near - field)
    zero = jnp.zeros((1,) + field.shape[1:], jnp.float32)
    above = jnp.concatenate([field[1:], zero], 0)
    above_wet = jnp.concatenate([wet[1:], zero], 0)
    below = jnp.concatenate([zero, field[:-1]], 0)
    below_wet = jnp.concatenate([zero, wet[:-1]], 0)
    vert = mixing * (above_wet * (above - field) + below_wet * (below - field))
    if stress is None:
        return field + wet * (horiz + vert)
    decay = jnp.exp(-level_index / 8.0)
    advect = 0.5 * decay * (stress[0] * (nears[0] - nears[1]) + stress[1] * (nears[2] - nears[3]))
    return field + wet * (horiz + vert - advect)


def split_rows(rows, cells_x, cells_y):
    row_part = rows // cells_y
    col_part = rows - row_part * cells_y
    pick_rows = (jnp.arange(cells_x, dtype=jnp.int32)[:, None] == row_part[None, :]).astype(
        jnp.float32
    )
    pick_cols = (jnp.arange(cells_y, dtype=jnp.int32)[:, None] == col_part[None, :]).astype(
        jnp.float32
    )
    return (pick_rows, pick_cols)


def on_device(state, coeffs, forcing, levels, remap):
    is_atm = lax.axis_index("sec") == 0
    field = state[0]
    coef = coeffs[0]
    depth_count = field.shape[0]
    cells_x = field.shape[1]
    cells_y = field.shape[2]
    depth = jnp.where(is_atm, jnp.float32(depth_count), levels.astype(jnp.float32))
    column = extended_2(jnp.stack([coef[0], depth]), ((TX, 1), (TY, 2)), 1)
    level_index = jnp.arange(depth_count, dtype=jnp.float32)[:, None, None]
    wet = (level_index < depth).astype(jnp.float32)
    atm = field
    for step in range(ASTEPS):
        heat = coef[2] * (atm[0] - forcing[3])
        atm = advance(atm, wet, column, coef[1], None)
        atm = atm.at[0].add(-heat)
    heat = coef[2] * (atm[0] - forcing[3])
    speed = jnp.sqrt(1.0 + forcing[0] * forcing[0] + forcing[1] * forcing[1])
    atm_flux = jnp.stack(
        [heat, forcing[2] - 0.5 * heat, 0.2 * speed * forcing[0], 0.2 * speed * forcing[1]]
    )
    links = remap.reshape(5, 9, CAP)

    def pick_block(sources):
        pick_rows, pick_cols = split_rows(sources, cells_x, cells_y)
        partial_rows = jnp.einsum(
            "cij,jb->cib", atm_flux, pick_cols, precision=lax.Precision.HIGHEST
        )
        return jnp.sum(partial_rows * pick_rows[None], 1)

    picked = lax.map(pick_block, links[0]).transpose(1, 0, 2)
    weight = links[4].astype(jnp.float32)
    payload = jnp.concatenate(
        [picked * weight[None], weight[None], links[3].astype(jnp.float32)[None]], 0
    )
    rows_n = lax.axis_size(TX)
    offsets = [(off_x, off_y) for off_x in (-1, 0, rows_n // 2) for off_y in (-1, 0, 1)]
    pieces = []
    for number, (off_x, off_y) in enumerate(offsets):
        piece = payload[:, number]
        if off_x != 0:
            piece = passed_along(piece, TX, off_x)
        if off_y != 0:
            piece = passed_along(piece, TY, off_y)
        pieces.append(piece)
    arrived = shifted(jnp.stack(pieces, 1), "sec", 1)

    def add_block(totals, block):
        pick_rows, pick_cols = split_rows(block[5].astype(jnp.int32), cells_x, cells_y)
        spread = block[:5][:, None, :] * pick_rows[None]
        return (
            totals + jnp.einsum("cib,jb->cij", spread, pick_cols, precision=lax.Precision.HIGHEST),
            None,
        )

    sums, unused = lax.scan(
        add_block, jnp.zeros((5, cells_x, cells_y), jnp.float32), arrived.transpose(1, 0, 2)
    )
    remapped = sums[:4] / jnp.maximum(sums[4], 1.0)
    surface = (levels > 0).astype(jnp.float32)
    ocean_side = 1.0 - is_atm.astype(jnp.float32)
    sent, received, count = (
        over_axes(jnp.sum(heat) * (1.0 - ocean_side), SEC_TX_TY),
        over_axes(jnp.sum(surface * remapped[0]) * ocean_side, SEC_TX_TY),
        over_axes(jnp.sum(surface) * ocean_side, SEC_TX_TY),
    )
    fix = (sent - received) / jnp.maximum(count, 1.0)
    ocean_flux = surface * jnp.stack([remapped[0] + fix, remapped[1], remapped[2], remapped[3]])
    ocean = field
    for step in range(OSTEPS):
        ocean = advance(ocean, wet, column, coef[1], (ocean_flux[2], ocean_flux[3]))
        ocean = ocean.at[0].add(surface * 4.0 * coef[2] * (ocean_flux[0] + 0.3 * ocean_flux[1]))
    new_state = jnp.where(is_atm, atm, ocean)[None]
    surface_flux = jnp.where(is_atm, atm_flux, ocean_flux)[None]
    return (new_state, surface_flux)


def solution(mesh):
    torus = Mesh(
        mesh.devices.reshape(mesh.shape["sec"], 4, 2, 2, 4), ("sec", "tx_0", "tx_1", "ty_0", "ty_1")
    )
    return jax.shard_map(
        on_device,
        mesh=torus,
        in_specs=(
            P("sec", None, TX, TY),
            P("sec", None, TX, TY),
            P(None, TX, TY),
            P(TX, TY),
            P(None, TX_TY),
        ),
        out_specs=(P("sec", None, TX, TY), P("sec", None, TX, TY)),
        check_vma=False,
    )
```

profile of v0, /device:TPU:0, one launch (start us, length us, event | category | flops | bytes accessed | tf_op | source)
XLA Modules:
  0.0 452.6 jit_solution(7034122351516204721)
XLA Ops:
  4.1 4.7 %collective-permute-start.3 = (f32[2,64,1]{2,1,0:T(8,128)S(1)}, f32[2,64,1]{2,1,0:T(8,128)S(1)}, u32[]{:S(2)}, u32[]{:S(2)}) collective-permute-start(f32[2,64,1]{2,1,0:T(8,128)S(1)} %get-tuple-element.278), channel_id=1, source_target_pairs={{1,0},{2,1},{3,2},{4,3},{5,4},{6,5},{7,6},{0,7},{9,8},{10,9},{11,1... | collective-permute-start | bytes 1544 | tf_op jit(solution)/shard_map/ppermute | solution.py:43
  10.1 2.7 collective-permute-start.2
  16.9 8.7 %slice_bitcast_fusion.1 = (f32[71,64,256]{2,1,0:T(8,128)}, f32[71,64,256]{2,1,0:T(8,128)}) fusion(f32[1,72,64,256]{3,2,1,0:T(8,128)} %param.19), kind=kLoop, calls=%fused_computation.141 | loop fusion | bytes 18612224 | tf_op jit(solution)/shard_map/slice | solution.py:88
  26.2 4.8 %fusion.118 = (f32[71,64,256]{2,1,0:T(8,128)}, f32[71,64,256]{2,1,0:T(8,128)}) fusion(f32[72,64,256]{2,1,0:T(8,128)S(1)} %fusion.81), kind=kLoop, calls=%fused_computation.250 | loop fusion | bytes 18612224 | tf_op jit(solution)/shard_map/slice | solution.py:89
  32.2 5.3 %collective-permute-done.5 = f32[72,1,256]{2,1,0:T(1,128)S(1)} collective-permute-done((f32[72,1,256]{2,1,0:T(1,128)S(1)}, f32[72,1,256]{2,1,0:T(1,128)S(1)}, u32[]{:S(2)}, u32[]{:S(2)}) %collective-permute-start.5) | collective-permute-done | bytes 73760 | tf_op jit(solution)/shard_map/ppermute | solution.py:25
  50.1 4.8 %collective-permute-done.7 = f32[72,66,1]{0,2,1:T(1,128)} collective-permute-done((f32[72,66,1]{0,2,1:T(1,128)}, f32[72,66,1]{0,2,1:T(1,128)}, u32[]{:S(2)}, u32[]{:S(2)}) %collective-permute-start.7) | collective-permute-done | bytes 19040 | tf_op jit(solution)/shard_map/ppermute | solution.py:25
  54.9 3.1 copy.60
  58.0 25.3 %select_add_fusion = (f32[72,64,256]{2,1,0:T(8,128)S(1)}, f32[72,64,256]{2,1,0:T(8,128)}) fusion(f32[64,256]{1,0:T(8,128)S(1)} %convert_select_fusion, f32[1,72,64,256]{3,2,1,0:T(8,128)} %param.19, f32[72,64,256]{2,1,0:T(8,128)} %bitcast.167, f32[71,64,256]{2,1,0:T(8,128)} %get-tuple-element.248, f32[71,64,256]{2,1,0:T(8,128)} %get-tuple-element.246, ...), kind=kLoop, calls=%fused_computation.129 | loop fusion | flops 48365568 | bytes 38327424 | tf_op jit(solution)/shard_map/add | solution.py:94
  87.0 3.8 slice_reduce_fusion
  101.2 8.7 %fusion.115 = (f32[71,64,256]{2,1,0:T(8,128)}, f32[71,64,256]{2,1,0:T(8,128)}) fusion(f32[72,64,256]{2,1,0:T(8,128)} %copy-done), kind=kLoop, calls=%fused_computation.247 | loop fusion | bytes 18612224 | tf_op jit(solution)/shard_map/slice | solution.py:88
  111.6 3.1 copy.64
  114.7 20.5 %fusion.57 = f32[72,64,256]{2,1,0:T(8,128)S(1)} fusion(f32[72,64,256]{2,1,0:T(8,128)} %copy-done, f32[72,66,1]{2,1,0:T(8,128)} %copy.64, f32[72,1,256]{2,1,0:T(1,128)} %copy-done.28, f32[72,1,256]{2,1,0:T(1,128)} %copy-done.30, f32[72,66,1]{2,1,0:T(8,128)S(1)} %copy.62, f32[71,64,256]{2,1,0:T(8,128)} %get-tuple-element.240, ...), kind=kLoop, calls=%fused_computation.89 | loop fusion | flops 48365568 | bytes 28890240 | tf_op jit(solution)/shard_map/add | solution.py:94
  147.6 2.9 pad_maximum_fusion.2
  155.5 4.6 %collective-permute-start.14 = (f32[72,66,1]{0,2,1:T(1,128)S(1)}, f32[72,66,1]{0,2,1:T(1,128)}, u32[]{:S(2)}, u32[]{:S(2)}) collective-permute-start(f32[72,66,1]{0,2,1:T(1,128)S(1)} %copy.65), channel_id=1, source_target_pairs={{1,0},{2,1},{3,2},{4,3},{5,4},{6,5},{7,6},{0,7},{9,8},{10,9},{11,1... | collective-permute-start | bytes 57032 | tf_op jit(solution)/shard_map/ppermute | solution.py:27
  161.6 8.6 %fusion.113 = (f32[71,64,256]{2,1,0:T(8,128)}, f32[71,64,256]{2,1,0:T(8,128)}) fusion(f32[72,64,256]{2,1,0:T(8,128)} %copy-done.1), kind=kLoop, calls=%fused_computation.245 | loop fusion | bytes 18612224 | tf_op jit(solution)/shard_map/slice | solution.py:88
  171.9 3.1 copy.68
  175.0 22.1 %fusion.43 = f32[72,64,256]{2,1,0:T(8,128)} fusion(f32[72,64,256]{2,1,0:T(8,128)} %copy-done.1, f32[72,66,1]{2,1,0:T(8,128)} %copy.68, f32[72,1,256]{2,1,0:T(1,128)} %copy-done.27, f32[72,1,256]{2,1,0:T(1,128)} %copy-done.29, f32[72,66,1]{2,1,0:T(8,128)S(1)} %copy.66, f32[71,64,256]{2,1,0:T(8,128)} %get-tuple-element.236, ...), kind=kLoop, calls=%fused_computation.67 | loop fusion | flops 48365568 | bytes 28890240 | tf_op jit(solution)/shard_map/add | solution.py:94
  200.0 37.1 %while.30 = (s32[]{:T(128)}, f32[9,4,4096]{2,1,0:T(4,128)}, s32[9,4096]{1,0:T(8,128)}, f32[4,64,256]{2,1,0:T(8,128)S(1)}, s32[]{:T(128)}) while((s32[]{:T(128)}, f32[9,4,4096]{2,1,0:T(4,128)}, s32[9,4096]{1,0:T(8,128)}, f32[4,64,256]{2,1,0:T(8,128)S(1)}, s32[]{:T(128)}) %tuple.131), condition=%wide.region_2.3_spmd, body=%wide.region_0.2_spmd.sunk | while | flops 3224948736 | bytes 2638401 | solution.py:142
  240.8 3.1 collective-permute-done.16
  243.9 8.4 %collective-permute-start.17 = (f32[6,4096]{1,0:T(8,128)S(1)}, f32[6,4096]{1,0:T(8,128)S(1)}, u32[]{:S(2)}, u32[]{:S(2)}) collective-permute-start(f32[6,4096]{1,0:T(8,128)S(1)} %collective-permute-done.16), channel_id=1, source_target_pairs={{0,7},{1,0},{2,1},{3,2},{4,3},{5,4},{6,5},{7,6},{8,15},{9,8},{10,9... | collective-permute-start | bytes 294920 | tf_op jit(solution)/shard_map/ppermute | solution.py:56
  252.3 2.9 collective-permute-start.18
  261.2 3.2 collective-permute-done.20
  266.4 3.5 collective-permute-start.26
  272.9 3.0 collective-permute-start.24
  280.6 3.9 collective-permute-done.27
  289.1 45.4 %while.31 = (s32[]{:T(128)}, f32[5,64,256]{2,1,0:T(8,128)}, f32[9,6,4096]{2,1,0:T(8,128)S(1)}, s32[]{:T(128)}, s32[]{:T(128)}, /*index=5*/s32[]{}) while((s32[]{:T(128)}, f32[5,64,256]{2,1,0:T(8,128)}, f32[9,6,4096]{2,1,0:T(8,128)S(1)}, s32[]{:T(128)}, s32[]{:T(128)}, /*index=5*/s32[]{}) %tuple.137), condition=%wide.region_4.5_spmd.clone, body=%wide.region_3.4_spmd.clone.sunk | while | flops 4029652992 | bytes 3113063 | solution.py:167
  289.3 4.0 fusion.138
  293.4 5.0 %fusion.138 = f32[5,64,256]{2,1,0:T(8,128)} fusion(s32[4096]{0:T(1024)S(1)} %get-tuple-element.338, f32[64,4096]{1,0:T(8,128)S(1)} %fusion.137, f32[5,4096]{1,0:T(8,128)S(1)} %dynamic-slice_bitcast_fusion.2, f32[5,64,256]{2,1,0:T(8,128)} %get-tuple-element.362, pred[]{:T(512)S(6)} %compare.80), kind=kOutput, calls=%fused_computation.21.clone.1 | convolution fusion | flops 4029054976 | bytes 1802241 | tf_op jit(solution)/shard_map/while/body/eval_jaxpr/cib,jb->cij/dot_general | solution.py:163
  298.6 5.0 %fusion.138 = f32[5,64,256]{2,1,0:T(8,128)} fusion(s32[4096]{0:T(1024)S(1)} %get-tuple-element.338, f32[64,4096]{1,0:T(8,128)S(1)} %fusion.137, f32[5,4096]{1,0:T(8,128)S(1)} %dynamic-slice_bitcast_fusion.2, f32[5,64,256]{2,1,0:T(8,128)} %get-tuple-element.362, pred[]{:T(512)S(6)} %compare.80), kind=kOutput, calls=%fused_computation.21.clone.1 | convolution fusion | flops 4029054976 | bytes 1802241 | tf_op jit(solution)/shard_map/while/body/eval_jaxpr/cib,jb->cij/dot_general | solution.py:163
  303.7 5.0 %fusion.138 = f32[5,64,256]{2,1,0:T(8,128)} fusion(s32[4096]{0:T(1024)S(1)} %get-tuple-element.338, f32[64,4096]{1,0:T(8,128)S(1)} %fusion.137, f32[5,4096]{1,0:T(8,128)S(1)} %dynamic-slice_bitcast_fusion.2, f32[5,64,256]{2,1,0:T(8,128)} %get-tuple-element.362, pred[]{:T(512)S(6)} %compare.80), kind=kOutput, calls=%fused_computation.21.clone.1 | convolution fusion | flops 4029054976 | bytes 1802241 | tf_op jit(solution)/shard_map/while/body/eval_jaxpr/cib,jb->cij/dot_general | solution.py:163
  308.9 5.0 %fusion.138 = f32[5,64,256]{2,1,0:T(8,128)} fusion(s32[4096]{0:T(1024)S(1)} %get-tuple-element.338, f32[64,4096]{1,0:T(8,128)S(1)} %fusion.137, f32[5,4096]{1,0:T(8,128)S(1)} %dynamic-slice_bitcast_fusion.2, f32[5,64,256]{2,1,0:T(8,128)} %get-tuple-element.362, pred[]{:T(512)S(6)} %compare.80), kind=kOutput, calls=%fused_computation.21.clone.1 | convolution fusion | flops 4029054976 | bytes 1802241 | tf_op jit(solution)/shard_map/while/body/eval_jaxpr/cib,jb->cij/dot_general | solution.py:163
  314.0 5.0 %fusion.138 = f32[5,64,256]{2,1,0:T(8,128)} fusion(s32[4096]{0:T(1024)S(1)} %get-tuple-element.338, f32[64,4096]{1,0:T(8,128)S(1)} %fusion.137, f32[5,4096]{1,0:T(8,128)S(1)} %dynamic-slice_bitcast_fusion.2, f32[5,64,256]{2,1,0:T(8,128)} %get-tuple-element.362, pred[]{:T(512)S(6)} %compare.80), kind=kOutput, calls=%fused_computation.21.clone.1 | convolution fusion | flops 4029054976 | bytes 1802241 | tf_op jit(solution)/shard_map/while/body/eval_jaxpr/cib,jb->cij/dot_general | solution.py:163
  319.2 5.0 %fusion.138 = f32[5,64,256]{2,1,0:T(8,128)} fusion(s32[4096]{0:T(1024)S(1)} %get-tuple-element.338, f32[64,4096]{1,0:T(8,128)S(1)} %fusion.137, f32[5,4096]{1,0:T(8,128)S(1)} %dynamic-slice_bitcast_fusion.2, f32[5,64,256]{2,1,0:T(8,128)} %get-tuple-element.362, pred[]{:T(512)S(6)} %compare.80), kind=kOutput, calls=%fused_computation.21.clone.1 | convolution fusion | flops 4029054976 | bytes 1802241 | tf_op jit(solution)/shard_map/while/body/eval_jaxpr/cib,jb->cij/dot_general | solution.py:163
  324.3 5.0 %fusion.138 = f32[5,64,256]{2,1,0:T(8,128)} fusion(s32[4096]{0:T(1024)S(1)} %get-tuple-element.338, f32[64,4096]{1,0:T(8,128)S(1)} %fusion.137, f32[5,4096]{1,0:T(8,128)S(1)} %dynamic-slice_bitcast_fusion.2, f32[5,64,256]{2,1,0:T(8,128)} %get-tuple-element.362, pred[]{:T(512)S(6)} %compare.80), kind=kOutput, calls=%fused_computation.21.clone.1 | convolution fusion | flops 4029054976 | bytes 1802241 | tf_op jit(solution)/shard_map/while/body/eval_jaxpr/cib,jb->cij/dot_general | solution.py:163
  329.5 5.0 %fusion.138 = f32[5,64,256]{2,1,0:T(8,128)} fusion(s32[4096]{0:T(1024)S(1)} %get-tuple-element.338, f32[64,4096]{1,0:T(8,128)S(1)} %fusion.137, f32[5,4096]{1,0:T(8,128)S(1)} %dynamic-slice_bitcast_fusion.2, f32[5,64,256]{2,1,0:T(8,128)} %get-tuple-element.362, pred[]{:T(512)S(6)} %compare.80), kind=kOutput, calls=%fused_computation.21.clone.1 | convolution fusion | flops 4029054976 | bytes 1802241 | tf_op jit(solution)/shard_map/while/body/eval_jaxpr/cib,jb->cij/dot_general | solution.py:163
  338.9 3.1 all-reduce.16
  342.0 9.1 %all-reduce.13 = (f32[]{:T(128)}, f32[]{:T(128)}, f32[]{:T(128)}) all-reduce(f32[]{:T(128)} %get-tuple-element.202, f32[]{:T(128)} %get-tuple-element.203, f32[]{:T(128)} %get-tuple-element.204), channel_id=1, replica_groups=mesh['sec'=2,'tx_0'=4,'tx_1'=2,'ty_0'=2,'ty_1'=4] {'tx_0'}, use_global_device_ids=true, to_apply=%region_7.8 | all-reduce | flops 3 | bytes 24 | tf_op jit(solution)/shard_map/psum | solution.py:66
  351.1 5.6 %all-reduce.15 = (f32[]{:T(128)}, f32[]{:T(128)}, f32[]{:T(128)}) all-reduce(f32[]{:T(128)} %get-tuple-element.193, f32[]{:T(128)} %get-tuple-element.194, f32[]{:T(128)} %get-tuple-element.195), channel_id=1, replica_groups=mesh['sec'=2,'tx_0'=4,'tx_1'=2,'ty_0'=2,'ty_1'=4] {'tx_1'}, use_global_device_ids=true, to_apply=%region_8.9 | all-reduce | flops 3 | bytes 24 | tf_op jit(solution)/shard_map/psum | solution.py:66
  356.7 7.1 %all-reduce.14 = (f32[]{:T(128)}, f32[]{:T(128)}, f32[]{:T(128)}) all-reduce(f32[]{:T(128)} %get-tuple-element.199, f32[]{:T(128)} %get-tuple-element.200, f32[]{:T(128)} %get-tuple-element.201), channel_id=1, replica_groups=mesh['sec'=2,'tx_0'=4,'tx_1'=2,'ty_0'=2,'ty_1'=4] {'ty_0'}, use_global_device_ids=true, to_apply=%region_9.10 | all-reduce | flops 3 | bytes 24 | tf_op jit(solution)/shard_map/psum | solution.py:66
  363.8 9.2 %all-reduce.12 = (f32[]{:T(128)}, f32[]{:T(128)}, f32[]{:T(128)}) all-reduce(f32[]{:T(128)} %get-tuple-element.196, f32[]{:T(128)} %get-tuple-element.197, f32[]{:T(128)} %get-tuple-element.198), channel_id=1, replica_groups=mesh['sec'=2,'tx_0'=4,'tx_1'=2,'ty_0'=2,'ty_1'=4] {'ty_1'}, use_global_device_ids=true, to_apply=%region_10.11 | all-reduce | flops 3 | bytes 24 | tf_op jit(solution)/shard_map/psum | solution.py:66
  375.1 15.7 %fusion.73 = f32[72,64,256]{2,1,0:T(8,128)S(1)} fusion(f32[72,64,256]{2,1,0:T(8,128)} %bitcast.168, f32[72,64,256]{2,1,0:T(8,128)} %get-tuple-element.220, f32[72,1,256]{2,1,0:T(1,128)S(1)} %copy-done.11, f32[72,1,256]{2,1,0:T(1,128)S(1)} %copy-done.9, f32[72,66,1]{2,1,0:T(8,128)} %copy-done.3, f32[72,66,1]{2,1,0:T(8,128)} %copy.60, ...), kind=kLoop, calls=%fused_computation.119 | loop fusion | flops 21233664 | bytes 14538144 | tf_op jit(solution)/shard_map/add | solution.py:97
  391.6 5.0 %fusion.111 = (f32[71,64,256]{2,1,0:T(8,128)}, f32[71,64,256]{2,1,0:T(8,128)}) fusion(f32[72,64,256]{2,1,0:T(8,128)S(1)} %get-tuple-element.207), kind=kLoop, calls=%fused_computation.243 | loop fusion | bytes 18612224 | tf_op jit(solution)/shard_map/slice | solution.py:88
  400.9 3.5 collective-permute-done.30
  410.9 3.4 collective-permute-start.31
  419.1 4.4 collective-permute-done.32
  423.5 3.1 copy.72
  426.7 20.0 %fusion.30 = f32[72,64,256]{2,1,0:T(8,128)S(1)} fusion(f32[72,64,256]{2,1,0:T(8,128)} %copy-done.2, f32[72,1,256]{2,1,0:T(1,128)} %copy-done.26, f32[72,1,256]{2,1,0:T(1,128)S(1)} %copy-done.25, f32[71,64,256]{2,1,0:T(8,128)} %get-tuple-element.232, f32[71,64,256]{2,1,0:T(8,128)} %get-tuple-element.231, f32[72,66,1]{2,1,0:T(8,128)} %copy.72, ...), kind=kLoop, calls=%fused_computation.52 | loop fusion | flops 56623104 | bytes 29021600 | tf_op jit(solution)/shard_map/add | solution.py:97
  446.7 5.4 %select_bitcast_fusion = f32[1,72,64,256]{3,2,1,0:T(8,128)} fusion(f32[72,64,256]{2,1,0:T(8,128)} %get-tuple-element.283, f32[72,64,256]{2,1,0:T(8,128)S(1)} %fusion.83, pred[]{:T(512)S(6)} %eq.87), kind=kLoop, calls=%fused_computation.128 | loop fusion | flops 1179648 | bytes 14155777 | tf_op jit(solution)/shard_map/broadcast_in_dim | solution.py:184
  (263 shorter events, 143.3 us)
Async XLA Ops:
  2.5 28.5 %collective-permute-start = (f32[2,64,1]{2,1,0:T(8,128)S(1)}, f32[2,64,1]{2,1,0:T(8,128)S(1)}, u32[]{:S(2)}, u32[]{:S(2)}) collective-permute-start(f32[2,64,1]{2,1,0:T(8,128)S(1)} %get-tuple-element.277), channel_id=1, source_target_pairs={{0,1},{1,2},{2,3},{3,4},{4,5},{5,6},{6,7},{7,0},{8,9},{9,10},{10,1... | collective-permute-start | bytes 1544 | tf_op jit(solution)/shard_map/ppermute | solution.py:42
  4.1 27.2 %collective-permute-start.3 = (f32[2,64,1]{2,1,0:T(8,128)S(1)}, f32[2,64,1]{2,1,0:T(8,128)S(1)}, u32[]{:S(2)}, u32[]{:S(2)}) collective-permute-start(f32[2,64,1]{2,1,0:T(8,128)S(1)} %get-tuple-element.278), channel_id=1, source_target_pairs={{1,0},{2,1},{3,2},{4,3},{5,4},{6,5},{7,6},{0,7},{9,8},{10,9},{11,1... | collective-permute-start | bytes 1544 | tf_op jit(solution)/shard_map/ppermute | solution.py:43
  8.7 22.5 %collective-permute-start.1 = (f32[2,1,256]{2,1,0:T(1,128)S(1)}, f32[2,1,256]{2,1,0:T(1,128)S(1)}, u32[]{:S(2)}, u32[]{:S(2)}) collective-permute-start(f32[2,1,256]{2,1,0:T(1,128)S(1)} %get-tuple-element.275), channel_id=1, source_target_pairs={{0,8},{8,16},{16,24},{24,32},{32,40},{40,48},{48,56},{56,0},{1,9},... | collective-permute-start | bytes 6152 | tf_op jit(solution)/shard_map/ppermute | solution.py:42
  10.1 21.1 %collective-permute-start.2 = (f32[2,1,256]{2,1,0:T(1,128)S(1)}, f32[2,1,256]{2,1,0:T(1,128)S(1)}, u32[]{:S(2)}, u32[]{:S(2)}) collective-permute-start(f32[2,1,256]{2,1,0:T(1,128)S(1)} %get-tuple-element.276), channel_id=1, source_target_pairs={{8,0},{16,8},{24,16},{32,24},{40,32},{48,40},{56,48},{0,56},{9,1},... | collective-permute-start | bytes 6152 | tf_op jit(solution)/shard_map/ppermute | solution.py:43
  14.2 17.9 %collective-permute-start.4 = (f32[72,1,256]{2,1,0:T(1,128)S(1)}, f32[72,1,256]{2,1,0:T(1,128)S(1)}, u32[]{:S(2)}, u32[]{:S(2)}) collective-permute-start(f32[72,1,256]{2,1,0:T(1,128)S(1)} %get-tuple-element.244), channel_id=1, source_target_pairs={{8,0},{16,8},{24,16},{32,24},{40,32},{48,40},{56,48},{0,56},{9,1},... | collective-permute-start | bytes 221192 | tf_op jit(solution)/shard_map/ppermute | solution.py:27
  31.0 6.5 %collective-permute-start.5 = (f32[72,1,256]{2,1,0:T(1,128)S(1)}, f32[72,1,256]{2,1,0:T(1,128)S(1)}, u32[]{:S(2)}, u32[]{:S(2)}) collective-permute-start(f32[72,1,256]{2,1,0:T(1,128)S(1)} %get-tuple-element.243), channel_id=1, source_target_pairs={{0,8},{8,16},{16,24},{24,32},{32,40},{40,48},{48,56},{56,0},{1,9},... | collective-permute-start | bytes 221192 | tf_op jit(solution)/shard_map/ppermute | solution.py:25
  43.2 5.2 %collective-permute-start.6 = (f32[72,66,1]{0,2,1:T(1,128)S(1)}, f32[72,66,1]{0,2,1:T(1,128)}, u32[]{:S(2)}, u32[]{:S(2)}) collective-permute-start(f32[72,66,1]{0,2,1:T(1,128)S(1)} %copy.57), channel_id=1, source_target_pairs={{1,0},{2,1},{3,2},{4,3},{5,4},{6,5},{7,6},{0,7},{9,8},{10,9},{11,1... | collective-permute-start | bytes 57032 | tf_op jit(solution)/shard_map/ppermute | solution.py:27
  46.8 8.0 %collective-permute-start.7 = (f32[72,66,1]{0,2,1:T(1,128)}, f32[72,66,1]{0,2,1:T(1,128)}, u32[]{:S(2)}, u32[]{:S(2)}) collective-permute-start(f32[72,66,1]{0,2,1:T(1,128)} %copy.59), channel_id=1, source_target_pairs={{0,1},{1,2},{2,3},{3,4},{4,5},{5,6},{6,7},{7,0},{8,9},{9,10},{10,1... | collective-permute-start | bytes 57032 | tf_op jit(solution)/shard_map/ppermute | solution.py:25
  50.1 33.1 %copy-start.3 = (f32[72,66,1]{2,1,0:T(8,128)}, f32[72,66,1]{2,1,0:T(8,128)S(1)}, u32[]{:S(2)}) copy-start(f32[72,66,1]{2,1,0:T(8,128)S(1)} %copy.58) | copy-start | bytes 57028
  84.9 5.9 %collective-permute-start.8 = (f32[72,1,256]{2,1,0:T(1,128)S(1)}, f32[72,1,256]{2,1,0:T(1,128)S(1)}, u32[]{:S(2)}, u32[]{:S(2)}) collective-permute-start(f32[72,1,256]{2,1,0:T(1,128)S(1)} %get-tuple-element.242), channel_id=1, source_target_pairs={{8,0},{16,8},{24,16},{32,24},{40,32},{48,40},{56,48},{0,56},{9,1},... | collective-permute-start | bytes 221192 | tf_op jit(solution)/shard_map/ppermute | solution.py:27
  85.0 6.5 %collective-permute-start.9 = (f32[72,1,256]{2,1,0:T(1,128)S(1)}, f32[72,1,256]{2,1,0:T(1,128)S(1)}, u32[]{:S(2)}, u32[]{:S(2)}) collective-permute-start(f32[72,1,256]{2,1,0:T(1,128)S(1)} %get-tuple-element.241), channel_id=1, source_target_pairs={{0,8},{8,16},{16,24},{24,32},{32,40},{40,48},{48,56},{56,0},{1,9},... | collective-permute-start | bytes 221192 | tf_op jit(solution)/shard_map/ppermute | solution.py:25
  97.3 12.6 %collective-permute-start.10 = (f32[72,66,1]{0,2,1:T(1,128)S(1)}, f32[72,66,1]{0,2,1:T(1,128)}, u32[]{:S(2)}, u32[]{:S(2)}) collective-permute-start(f32[72,66,1]{0,2,1:T(1,128)S(1)} %copy.61), channel_id=1, source_target_pairs={{1,0},{2,1},{3,2},{4,3},{5,4},{6,5},{7,6},{0,7},{9,8},{10,9},{11,1... | collective-permute-start | bytes 57032 | tf_op jit(solution)/shard_map/ppermute | solution.py:27
  99.7 11.9 %collective-permute-start.11 = (f32[72,66,1]{0,2,1:T(1,128)}, f32[72,66,1]{0,2,1:T(1,128)}, u32[]{:S(2)}, u32[]{:S(2)}) collective-permute-start(f32[72,66,1]{0,2,1:T(1,128)} %copy.63), channel_id=1, source_target_pairs={{0,1},{1,2},{2,3},{3,4},{4,5},{5,6},{6,7},{7,0},{8,9},{9,10},{10,1... | collective-permute-start | bytes 57032 | tf_op jit(solution)/shard_map/ppermute | solution.py:25
  114.7 20.5 %copy-start.33 = (f32[1,64,256]{2,1,0:T(8,128)S(1)}, f32[1,64,256]{2,1,0:T(8,128)}, u32[]{:S(2)}) copy-start(f32[1,64,256]{2,1,0:T(8,128)} %get-tuple-element.218) | copy-start | bytes 196612
  139.0 6.2 %collective-permute-start.12 = (f32[72,1,256]{2,1,0:T(1,128)S(1)}, f32[72,1,256]{2,1,0:T(1,128)S(1)}, u32[]{:S(2)}, u32[]{:S(2)}) collective-permute-start(f32[72,1,256]{2,1,0:T(1,128)S(1)} %get-tuple-element.238), channel_id=1, source_target_pairs={{8,0},{16,8},{24,16},{32,24},{40,32},{48,40},{56,48},{0,56},{9,1},... | collective-permute-start | bytes 221192 | tf_op jit(solution)/shard_map/ppermute | solution.py:27
  140.5 6.5 %collective-permute-start.13 = (f32[72,1,256]{2,1,0:T(1,128)S(1)}, f32[72,1,256]{2,1,0:T(1,128)S(1)}, u32[]{:S(2)}, u32[]{:S(2)}) collective-permute-start(f32[72,1,256]{2,1,0:T(1,128)S(1)} %get-tuple-element.237), channel_id=1, source_target_pairs={{0,8},{8,16},{16,24},{24,32},{32,40},{40,48},{48,56},{56,0},{1,9},... | collective-permute-start | bytes 221192 | tf_op jit(solution)/shard_map/ppermute | solution.py:25
  155.5 14.8 %collective-permute-start.14 = (f32[72,66,1]{0,2,1:T(1,128)S(1)}, f32[72,66,1]{0,2,1:T(1,128)}, u32[]{:S(2)}, u32[]{:S(2)}) collective-permute-start(f32[72,66,1]{0,2,1:T(1,128)S(1)} %copy.65), channel_id=1, source_target_pairs={{1,0},{2,1},{3,2},{4,3},{5,4},{6,5},{7,6},{0,7},{9,8},{10,9},{11,1... | collective-permute-start | bytes 57032 | tf_op jit(solution)/shard_map/ppermute | solution.py:27
  161.4 10.5 %collective-permute-start.15 = (f32[72,66,1]{0,2,1:T(1,128)}, f32[72,66,1]{0,2,1:T(1,128)}, u32[]{:S(2)}, u32[]{:S(2)}) collective-permute-start(f32[72,66,1]{0,2,1:T(1,128)} %copy.67), channel_id=1, source_target_pairs={{0,1},{1,2},{2,3},{3,4},{4,5},{5,6},{6,7},{7,0},{8,9},{9,10},{10,1... | collective-permute-start | bytes 57032 | tf_op jit(solution)/shard_map/ppermute | solution.py:25
  175.0 22.1 %copy-start.6 = (f32[4,64,256]{2,1,0:T(8,128)S(1)}, f32[4,64,256]{2,1,0:T(8,128)}, u32[]{:S(2)}) copy-start(f32[4,64,256]{2,1,0:T(8,128)} %param.21) | copy-start | bytes 786436
  175.0 22.1 %copy-start.32 = (f32[1,64,256]{2,1,0:T(8,128)S(1)}, f32[1,64,256]{2,1,0:T(8,128)}, u32[]{:S(2)}) copy-start(f32[1,64,256]{2,1,0:T(8,128)} %get-tuple-element.216) | copy-start | bytes 196612
  199.9 37.2 %copy-start.5 = (f32[9,4096]{1,0:T(8,128)S(1)}, f32[9,4096]{1,0:T(8,128)}, u32[]{:S(2)}) copy-start(f32[9,4096]{1,0:T(8,128)} %convert_element_type.110) | copy-start | bytes 442372
  199.9 38.5 %copy-start.16 = (f32[1,36864]{1,0:T(1,128)S(1)}, f32[1,36864]{1,0:T(1,128)}, u32[]{:S(2)}) copy-start(f32[1,36864]{1,0:T(1,128)} %get-tuple-element.259) | copy-start | bytes 442372
  199.9 38.5 %copy-start.17 = (f32[1,36864]{1,0:T(1,128)S(1)}, f32[1,36864]{1,0:T(1,128)}, u32[]{:S(2)}) copy-start(f32[1,36864]{1,0:T(1,128)} %get-tuple-element.260) | copy-start | bytes 442372
  237.1 49.4 %copy-start.19 = (s32[64,256]{1,0:T(8,128)S(1)}, s32[64,256]{1,0:T(8,128)}, u32[]{:S(2)}) copy-start(s32[64,256]{1,0:T(8,128)} %param.22) | copy-start | bytes 196612
  238.8 5.0 %collective-permute-start.16 = (f32[6,4096]{1,0:T(8,128)S(1)}, f32[6,4096]{1,0:T(8,128)S(1)}, u32[]{:S(2)}, u32[]{:S(2)}) collective-permute-start(f32[6,4096]{1,0:T(8,128)S(1)} %get-tuple-element.257), channel_id=1, source_target_pairs={{0,56},{8,0},{16,8},{24,16},{32,24},{40,32},{48,40},{56,48},{1,57}... | collective-permute-start | bytes 294920 | tf_op jit(solution)/shard_map/ppermute | solution.py:56
  240.7 15.1 %collective-permute-start.19 = (f32[6,4096]{1,0:T(8,128)S(1)}, f32[6,4096]{1,0:T(8,128)S(1)}, u32[]{:S(2)}, u32[]{:S(2)}) collective-permute-start(f32[6,4096]{1,0:T(8,128)S(1)} %get-tuple-element.255), channel_id=1, source_target_pairs={{0,56},{8,0},{16,8},{24,16},{32,24},{40,32},{48,40},{56,48},{1,57}... | collective-permute-start | bytes 294920 | tf_op jit(solution)/shard_map/ppermute | solution.py:56
  243.9 13.4 %collective-permute-start.17 = (f32[6,4096]{1,0:T(8,128)S(1)}, f32[6,4096]{1,0:T(8,128)S(1)}, u32[]{:S(2)}, u32[]{:S(2)}) collective-permute-start(f32[6,4096]{1,0:T(8,128)S(1)} %collective-permute-done.16), channel_id=1, source_target_pairs={{0,7},{1,0},{2,1},{3,2},{4,3},{5,4},{6,5},{7,6},{8,15},{9,8},{10,9... | collective-permute-start | bytes 294920 | tf_op jit(solution)/shard_map/ppermute | solution.py:56
  252.3 8.2 %collective-permute-start.18 = (f32[6,4096]{1,0:T(8,128)S(1)}, f32[6,4096]{1,0:T(8,128)S(1)}, u32[]{:S(2)}, u32[]{:S(2)}) collective-permute-start(f32[6,4096]{1,0:T(8,128)S(1)} %get-tuple-element.256), channel_id=1, source_target_pairs={{0,56},{8,0},{16,8},{24,16},{32,24},{40,32},{48,40},{56,48},{1,57}... | collective-permute-start | bytes 294920 | tf_op jit(solution)/shard_map/ppermute | solution.py:56
  255.2 9.9 %collective-permute-start.21 = (f32[6,4096]{1,0:T(8,128)S(1)}, f32[6,4096]{1,0:T(8,128)S(1)}, u32[]{:S(2)}, u32[]{:S(2)}) collective-permute-start(f32[6,4096]{1,0:T(8,128)S(1)} %get-tuple-element.254), channel_id=1, source_target_pairs={{0,7},{1,0},{2,1},{3,2},{4,3},{5,4},{6,5},{7,6},{8,15},{9,8},{10,9... | collective-permute-start | bytes 294920 | tf_op jit(solution)/shard_map/ppermute | solution.py:56
  255.8 8.6 %collective-permute-start.20 = (f32[6,4096]{1,0:T(8,128)S(1)}, f32[6,4096]{1,0:T(8,128)S(1)}, u32[]{:S(2)}, u32[]{:S(2)}) collective-permute-start(f32[6,4096]{1,0:T(8,128)S(1)} %collective-permute-done.19), channel_id=1, source_target_pairs={{0,1},{1,2},{2,3},{3,4},{4,5},{5,6},{6,7},{7,0},{8,9},{9,10},{10,1... | collective-permute-start | bytes 294920 | tf_op jit(solution)/shard_map/ppermute | solution.py:56
  266.4 6.5 %collective-permute-start.23 = (f32[6,4096]{1,0:T(8,128)S(1)}, f32[6,4096]{1,0:T(8,128)S(1)}, u32[]{:S(2)}, u32[]{:S(2)}) collective-permute-start(f32[6,4096]{1,0:T(8,128)S(1)} %get-tuple-element.251), channel_id=1, source_target_pairs={{0,32},{8,40},{16,48},{24,56},{32,0},{40,8},{48,16},{56,24},{1,33}... | collective-permute-start | bytes 294920 | tf_op jit(solution)/shard_map/ppermute | solution.py:56
  266.4 9.5 %collective-permute-start.26 = (f32[6,4096]{1,0:T(8,128)S(1)}, f32[6,4096]{1,0:T(8,128)S(1)}, u32[]{:S(2)}, u32[]{:S(2)}) collective-permute-start(f32[6,4096]{1,0:T(8,128)S(1)} %get-tuple-element.249), channel_id=1, source_target_pairs={{0,32},{8,40},{16,48},{24,56},{32,0},{40,8},{48,16},{56,24},{1,33}... | collective-permute-start | bytes 294920 | tf_op jit(solution)/shard_map/ppermute | solution.py:56
  270.0 8.6 %collective-permute-start.22 = (f32[6,4096]{1,0:T(8,128)S(1)}, f32[6,4096]{1,0:T(8,128)S(1)}, u32[]{:S(2)}, u32[]{:S(2)}) collective-permute-start(f32[6,4096]{1,0:T(8,128)S(1)} %get-tuple-element.252), channel_id=1, source_target_pairs={{0,1},{1,2},{2,3},{3,4},{4,5},{5,6},{6,7},{7,0},{8,9},{9,10},{10,1... | collective-permute-start | bytes 294920 | tf_op jit(solution)/shard_map/ppermute | solution.py:56
  270.0 9.9 %collective-permute-start.25 = (f32[6,4096]{1,0:T(8,128)S(1)}, f32[6,4096]{1,0:T(8,128)S(1)}, u32[]{:S(2)}, u32[]{:S(2)}) collective-permute-start(f32[6,4096]{1,0:T(8,128)S(1)} %get-tuple-element.250), channel_id=1, source_target_pairs={{0,32},{8,40},{16,48},{24,56},{32,0},{40,8},{48,16},{56,24},{1,33}... | collective-permute-start | bytes 294920 | tf_op jit(solution)/shard_map/ppermute | solution.py:56
  272.9 6.3 %collective-permute-start.24 = (f32[6,4096]{1,0:T(8,128)S(1)}, f32[6,4096]{1,0:T(8,128)S(1)}, u32[]{:S(2)}, u32[]{:S(2)}) collective-permute-start(f32[6,4096]{1,0:T(8,128)S(1)} %collective-permute-done.23), channel_id=1, source_target_pairs={{0,7},{1,0},{2,1},{3,2},{4,3},{5,4},{6,5},{7,6},{8,15},{9,8},{10,9... | collective-permute-start | bytes 294920 | tf_op jit(solution)/shard_map/ppermute | solution.py:56
  275.9 8.6 %collective-permute-start.27 = (f32[6,4096]{1,0:T(8,128)S(1)}, f32[6,4096]{1,0:T(8,128)S(1)}, u32[]{:S(2)}, u32[]{:S(2)}) collective-permute-start(f32[6,4096]{1,0:T(8,128)S(1)} %collective-permute-done.26), channel_id=1, source_target_pairs={{0,1},{1,2},{2,3},{3,4},{4,5},{5,6},{6,7},{7,0},{8,9},{9,10},{10,1... | collective-permute-start | bytes 294920 | tf_op jit(solution)/shard_map/ppermute | solution.py:56
  285.1 4.0 collective-permute-start.28
  286.6 88.5 %copy-start.18 = (f32[64,256]{1,0:T(8,128)}, f32[64,256]{1,0:T(8,128)S(1)}, u32[]{:S(2)}) copy-start(f32[64,256]{1,0:T(8,128)S(1)} %get-tuple-element.209) | copy-start | bytes 196612
  289.1 86.0 %copy-start.9 = (f32[72,1,256]{2,1,0:T(1,128)S(1)}, f32[72,1,256]{2,1,0:T(1,128)}, u32[]{:S(2)}) copy-start(f32[72,1,256]{2,1,0:T(1,128)} %copy-done.8) | copy-start | bytes 221188
  289.1 86.0 %copy-start.11 = (f32[72,1,256]{2,1,0:T(1,128)S(1)}, f32[72,1,256]{2,1,0:T(1,128)}, u32[]{:S(2)}) copy-start(f32[72,1,256]{2,1,0:T(1,128)} %copy-done.10) | copy-start | bytes 221188
  375.1 15.8 %copy-start.12 = (f32[64,256]{1,0:T(8,128)}, f32[64,256]{1,0:T(8,128)S(1)}, u32[]{:S(2)}) copy-start(f32[64,256]{1,0:T(8,128)S(1)} %get-tuple-element.267) | copy-start | bytes 196612
  375.1 15.8 %copy-start.14 = (f32[64,256]{1,0:T(8,128)}, f32[64,256]{1,0:T(8,128)S(1)}, u32[]{:S(2)}) copy-start(f32[64,256]{1,0:T(8,128)S(1)} %get-tuple-element.268) | copy-start | bytes 196612
  391.5 13.0 %copy-start.2 = (f32[72,64,256]{2,1,0:T(8,128)}, f32[72,64,256]{2,1,0:T(8,128)S(1)}, u32[]{:S(2)}) copy-start(f32[72,64,256]{2,1,0:T(8,128)S(1)} %get-tuple-element.207) | copy-start | bytes 14155780
  396.6 4.4 collective-permute-start.29
  398.0 6.5 %collective-permute-start.30 = (f32[72,1,256]{2,1,0:T(1,128)S(1)}, f32[72,1,256]{2,1,0:T(1,128)S(1)}, u32[]{:S(2)}, u32[]{:S(2)}) collective-permute-start(f32[72,1,256]{2,1,0:T(1,128)S(1)} %get-tuple-element.234), channel_id=1, source_target_pairs={{0,8},{8,16},{16,24},{24,32},{32,40},{40,48},{48,56},{56,0},{1,9},... | collective-permute-start | bytes 221192 | tf_op jit(solution)/shard_map/ppermute | solution.py:25
  410.9 6.6 %collective-permute-start.31 = (f32[72,66,1]{0,2,1:T(1,128)S(1)}, f32[72,66,1]{0,2,1:T(1,128)}, u32[]{:S(2)}, u32[]{:S(2)}) collective-permute-start(f32[72,66,1]{0,2,1:T(1,128)S(1)} %copy.69), channel_id=1, source_target_pairs={{1,0},{2,1},{3,2},{4,3},{5,4},{6,5},{7,6},{0,7},{9,8},{10,9},{11,1... | collective-permute-start | bytes 57032 | tf_op jit(solution)/shard_map/ppermute | solution.py:27
  415.7 7.9 %collective-permute-start.32 = (f32[72,66,1]{0,2,1:T(1,128)}, f32[72,66,1]{0,2,1:T(1,128)}, u32[]{:S(2)}, u32[]{:S(2)}) collective-permute-start(f32[72,66,1]{0,2,1:T(1,128)} %copy.71), channel_id=1, source_target_pairs={{0,1},{1,2},{2,3},{3,4},{4,5},{5,6},{6,7},{7,0},{8,9},{9,10},{10,1... | collective-permute-start | bytes 57032 | tf_op jit(solution)/shard_map/ppermute | solution.py:25
  426.7 20.0 %copy-start.31 = (f32[1,64,256]{2,1,0:T(8,128)S(1)}, f32[1,64,256]{2,1,0:T(8,128)}, u32[]{:S(2)}) copy-start(f32[1,64,256]{2,1,0:T(8,128)} %get-tuple-element.208) | copy-start | bytes 196612
  (21 other events, 93.3 us)
where the time goes:
time: 461 us; the launch traced here: 453 us
  other arithmetic  147 us (32%)
  local copies, waits for them, and re-layouts  103 us (22%)
  matrix products  65.3 us (14%)
  starting transfers between devices  55.2 us (12%)
  waiting for transfers between devices  42.3 us (9%)
  blocking collectives  34.1 us (7%)
  between operations  5.53 us (1%)
    add x3, other arithmetic, advance(): return field + wet * (horiz + vert)  67.8 us
    dot_general x9, matrix products, add_block(): jnp.einsum('cib,jb->cij', spread, pick_cols, precision=lax.Precision.HIGH...  43.8 us
    add x2, other arithmetic, advance(): return field + wet * (horiz + vert - advect)  35.7 us
    psum x5, blocking collectives, over_axes(): return functools.reduce(lax.psum, axes, array)  34.1 us
    slice x4, local copies, waits for them, and re-layouts, advance(): above = jnp.concatenate([field[1:], zero], 0)  31 us
    ppermute x12, starting transfers between devices, passed_along(): lax.ppermute(array, axis, [(i, (i + by) % size) for i in range(size)])  22.1 us
    dot_general x9, matrix products, pick_block(): jnp.einsum('cij,jb->cib', atm_flux, pick_cols, precision=lax.Precision.HI...  21.5 us
    ppermute x8, waiting for transfers between devices, extended(): lax.ppermute(tail, axis, [(i, (i + 1) % count) for i in range(count)])  20.5 us
  transfers between devices with their start and end apart: 33, of which 14 were waited for; matrix products, arithmetic and copies ran while one was open for 14% of the time, Pallas kernels for 0%

commit v1 on v0

v1 whole, which is shorter than its diff:
```python
import math

import jax
import jax.numpy as jnp
from jax import lax
from jax.experimental import pallas as pl
from jax.experimental.pallas import tpu as pltpu
from jax.sharding import PartitionSpec as P

LEV, OLEV, CX, CY = 72, 60, 64, 256
CAP = 4096
TAB = 8
CH = 24
NCH = LEV // CH
F32, BF16 = jnp.float32, jnp.bfloat16
MESH = pl.DeviceIdType.MESH


def hi_lo(x):
    high = x.astype(BF16)
    return high, (x - high.astype(F32)).astype(BF16)


def wide(x, count):
    return jnp.concatenate([x] * count, 1)


def kernel(
    state, coef, forc, lev, remap, out_state, out_flux,
    buf, rsend, csend, rrecv, crecv, cf, lnk_s, lnk_r, val_s, val_r, acc, fb, iota, dec,
    rem, hst, qb, qrow, qcol, red, red1, red2,
    in_sem, out_sem, hs_sem, hr_sem, ls_sem, lr_sem, vs_sem, vr_sem, rs_sem, rr_sem,
    qs_sem, qr_sem, p1s_sem, p1r_sem, p2s_sem, p2r_sem,
):
    sec, tx, ty = lax.axis_index("sec"), lax.axis_index("tx"), lax.axis_index("ty")
    is_atm = sec == 0
    is_ocn = sec == 1

    def near(dx, dy):
        return (sec, lax.rem(tx + dx + 8, 8), lax.rem(ty + dy + 8, 8))

    barrier = pltpu.get_barrier_semaphore()
    for dx in (-1, 0, 1, 4):
        for dy in (-1, 0, 1):
            if dx != 0 or dy != 0:
                pl.semaphore_signal(barrier, 1, device_id=near(dx, dy), device_id_type=MESH)
    for dy in range(2, 7):
        pl.semaphore_signal(barrier, 1, device_id=near(0, dy), device_id_type=MESH)
    for dx in range(8):
        pl.semaphore_signal(
            barrier, 1, device_id=(1 - sec, lax.rem(tx + dx, 8), ty), device_id_type=MESH
        )

    def state_in(ch):
        return pltpu.make_async_copy(
            state.at[0, pl.ds(ch * CH, CH)],
            buf.at[0, pl.ds(ch * CH, CH), pl.ds(TAB, CX)],
            in_sem.at[ch],
        )

    for ch in range(NCH):
        state_in(ch).start()

    for n in range(9):
        lnk_s[n] = remap[3:5, n * CAP : (n + 1) * CAP]
    iota[...] = lax.broadcasted_iota(jnp.int32, (CY, 128), 0).astype(F32).astype(BF16)
    dec[...] = 0.5 * jnp.exp(lax.broadcasted_iota(jnp.int32, (LEV, 128), 0).astype(F32) * (-1 / 8))
    lane = lax.broadcasted_iota(jnp.int32, (8, 128), 1)

    kap, mix, c2 = coef[0, 0], coef[0, 1], coef[0, 2]
    depth = jnp.where(is_atm, jnp.full((CX, CY), float(LEV), F32), lev[...].astype(F32))
    surface = (lev[...] > 0).astype(F32)

    pl.semaphore_wait(barrier, 24)

    def target_of(n):
        row_step = n // 3
        return near(row_step - 1 + 3 * (row_step // 2), n % 3 - 1)

    def lnk_copy(n):
        return pltpu.make_async_remote_copy(
            lnk_s.at[n], lnk_r.at[n], ls_sem.at[n], lr_sem.at[n],
            device_id=target_of(n), device_id_type=MESH,
        )

    def val_copy(n):
        return pltpu.make_async_remote_copy(
            val_s.at[n], val_r.at[n], vs_sem.at[n], vr_sem.at[n],
            device_id=target_of(n), device_id_type=MESH,
        )

    def halo_copies(s, ch):
        out = []
        for d, (there, low) in enumerate(
            ((near(1, 0), 0), (near(-1, 0), 1), (near(0, 1), 0), (near(0, -1), 1))
        ):
            send, recv = (rsend, rrecv) if d < 2 else (csend, crecv)
            out.append(
                pltpu.make_async_remote_copy(
                    send.at[s, ch, low], recv.at[s, ch, low],
                    hs_sem.at[s, ch, d], hr_sem.at[s, ch, d],
                    device_id=there, device_id_type=MESH,
                )
            )
        return out

    def pack_low(value, k):
        return pltpu.roll(value[:, :128], k, 1)

    def pack_high(value, k):
        return pltpu.roll(value[:, 128:], k + 1, 1)

    rsend[0, 0, 0, CH : CH + 8] = jnp.zeros((8, CY), F32)
    rsend[0, 0, 1, CH : CH + 8] = jnp.zeros((8, CY), F32)
    for at, plane in enumerate((kap, depth, c2)):
        rsend[0, 0, 0, CH + at : CH + at + 1] = plane[CX - 1 : CX]
        rsend[0, 0, 1, CH + at : CH + at + 1] = plane[0:1]
    for ch in range(NCH):
        state_in(ch).wait()

        def row_edges(kk, carry, ch=ch):
            k = ch * CH + kk
            rsend[0, ch, 0, pl.ds(kk, 1)] = buf[0, k, TAB + CX - 1 : TAB + CX]
            rsend[0, ch, 1, pl.ds(kk, 1)] = buf[0, k, TAB : TAB + 1]
            return carry

        lax.fori_loop(0, CH, row_edges, 0, unroll=8)
        for g in range(8):
            rows = slice(TAB + 8 * g, TAB + 8 * g + 8)

            def col_edges(kk, packs, ch=ch, rows=rows):
                value = buf[0, ch * CH + kk, rows]
                here = lane == kk
                return (
                    jnp.where(here, pack_high(value, kk), packs[0]),
                    jnp.where(here, pack_low(value, kk), packs[1]),
                )

            zero = jnp.zeros((8, 128), F32)
            packs = lax.fori_loop(0, CH, col_edges, (zero, zero), unroll=4)
            if ch == 0:
                for at, plane in enumerate((kap, depth, c2)):
                    part = plane[8 * g : 8 * g + 8]
                    packs = (
                        jnp.where(lane == CH + at, pack_high(part, CH + at), packs[0]),
                        jnp.where(lane == CH + at, pack_low(part, CH + at), packs[1]),
                    )
            csend[0, ch, 0, 8 * g : 8 * g + 8] = packs[0]
            csend[0, ch, 1, 8 * g : 8 * g + 8] = packs[1]
        for copy in halo_copies(0, ch):
            copy.start()

    for n in range(9):
        if n != 4:
            lnk_copy(n).start()

    lane_all = lax.broadcasted_iota(jnp.int32, (CX, CY), 1)

    def shifted(plane, at):
        low_row = rrecv[0, 0, 0, CH + at : CH + at + 1]
        high_row = rrecv[0, 0, 1, CH + at : CH + at + 1]
        low_col = crecv[0, 0, 0][:, CH + at : CH + at + 1]
        high_col = crecv[0, 0, 1][:, CH + at : CH + at + 1]
        return (
            jnp.concatenate([low_row, plane[:-1]], 0),
            jnp.concatenate([plane[1:], high_row], 0),
            jnp.where(lane_all == 0, low_col, pltpu.roll(plane, 1, 1)),
            jnp.where(lane_all == CY - 1, high_col, pltpu.roll(plane, CY - 1, 1)),
        )

    def static_part():
        total = jnp.zeros((CX, CY), F32)
        for at, other in enumerate(shifted(kap, 0)):
            half = 0.5 * (kap + other)
            cf[at] = half
            total = total + half
        cf[4] = mix
        cf[5] = (1.0 - total) - 2.0 * mix

    def halos_arrived(s, ch):
        for copy in halo_copies(s, ch):
            copy.wait_recv()

        @pl.when(jnp.logical_and(s == 0, ch == 0))
        def _():
            static_part()
            for at, other in enumerate(shifted(depth, 1)):
                cf[6 + at] = other

    def rows_in(s, slot, ch, count):
        def one(kk, carry):
            k = ch * CH + kk
            buf[slot, k, TAB - 1 : TAB] = rrecv[s, ch, 0, pl.ds(kk, 1)]
            buf[slot, k, TAB + CX : TAB + CX + 1] = rrecv[s, ch, 1, pl.ds(kk, 1)]
            return carry

        lax.fori_loop(0, count, one, 0, unroll=4)

    lane_wide = lax.broadcasted_iota(jnp.int32, (8, CY), 1)

    def sides(slot, k, kk, g, value, col_low, col_high):
        at = TAB + 8 * g
        up = buf[slot, k, at - 1 : at + 7]
        down = buf[slot, k, at + 1 : at + 9]
        back = lax.rem(128 - kk, 128)
        low = pltpu.roll(col_low, back, 1)
        high = pltpu.roll(col_high, lax.rem(127 - kk + 128, 128), 1)
        left = jnp.where(lane_wide == 0, wide(low, 2), pltpu.roll(value, 1, 1))
        right = jnp.where(lane_wide == CY - 1, wide(high, 2), pltpu.roll(value, CY - 1, 1))
        return up, down, left, right

    @pl.when(is_atm)
    def _():
        def piece(t, carry):
            s, ch = t // NCH, t % NCH
            slot = s % 2
            halos_arrived(s, ch)
            rows_in(s, slot, ch, CH)
            first = ch * CH
            after = s + 1
            for g in range(8):
                part = slice(8 * g, 8 * g + 8)
                rows = slice(TAB + 8 * g, TAB + 8 * g + 8)
                c_up, c_down, c_left, c_right, c_mix, c_own = [cf[i, part] for i in range(6)]
                col_low, col_high = crecv[s, ch, 0, part], crecv[s, ch, 1, part]
                top = buf[slot, 0, rows]
                heat = coef[0, 2, part] * (top - forc[3, part])
                extra = jnp.where(ch == 0, -heat, 0.0)

                def level(kk, held):
                    before, value, extra, pack0, pack1 = held
                    k = first + kk
                    following = buf[slot, jnp.minimum(k + 1, LEV - 1), rows]
                    up, down, left, right = sides(slot, k, kk, g, value, col_low, col_high)
                    new = (c_own * value + extra) + c_mix * (before + following)
                    new = new + (c_up * up + c_down * down) + (c_left * left + c_right * right)
                    buf[1 - slot, k, rows] = new
                    here = lane == kk
                    pack0 = jnp.where(here, pack_high(new, kk), pack0)
                    pack1 = jnp.where(here, pack_low(new, kk), pack1)
                    if g == 7:
                        rsend[after, ch, 0, pl.ds(kk, 1)] = new[7:8]
                    if g == 0:
                        rsend[after, ch, 1, pl.ds(kk, 1)] = new[0:1]
                    return value, following, jnp.zeros_like(extra), pack0, pack1

                zero = jnp.zeros((8, 128), F32)
                held = (buf[slot, jnp.maximum(first - 1, 0), rows], buf[slot, first, rows], extra, zero, zero)
                held = lax.fori_loop(0, CH, level, held, unroll=4)
                csend[after, ch, 0, part] = held[3]
                csend[after, ch, 1, part] = held[4]

            @pl.when(s < 2)
            def _():
                for copy in halo_copies(after, ch):
                    copy.start()

            return carry

        lax.fori_loop(0, 3 * NCH, piece, 0)
        pltpu.make_async_copy(buf.at[1, :, pl.ds(TAB, CX)], out_state.at[0], out_sem).start()
        heat = c2 * (buf[1, 0, TAB : TAB + CX] - forc[3])
        out_flux[0, 0] = heat
        out_flux[0, 1] = forc[2] - 0.5 * heat

    speed = 0.2 * jnp.sqrt(1.0 + forc[0] * forc[0] + forc[1] * forc[1])

    @pl.when(is_atm)
    def _():
        out_flux[0, 2] = speed * forc[0]
        out_flux[0, 3] = speed * forc[1]

    @pl.when(is_ocn)
    def _():
        out_flux[0, 0] = speed * forc[0]
        out_flux[0, 1] = speed * forc[1]

    for c in range(2):
        high, low = hi_lo(out_flux[0, c])
        fb[CX * c : CX * (c + 1)] = high
        fb[2 * CX + CX * c : 2 * CX + CX * (c + 1)] = low
    one, none = jnp.array(1, BF16), jnp.array(0, BF16)

    def pick(t, carry):
        n = lax.rem(t + 5, 9)
        at = pl.multiple_of(n * CAP, CAP)
        source = remap[0:1, pl.ds(at, CAP)]
        weight = remap[4:5, pl.ds(at, CAP)].astype(F32)
        col = (source & (CY - 1)).astype(F32).astype(BF16)
        hot = jnp.where(wide(iota[...], CAP // 128) == col, one, none)
        product = jnp.dot(fb[...], hot, preferred_element_type=F32)
        here = lax.broadcasted_iota(jnp.int32, (CX, CAP), 0) == (source >> 8)
        for c in range(2):
            both = product[CX * c : CX * (c + 1)] + product[2 * CX + CX * c : 2 * CX + CX * (c + 1)]
            val_s[n, c : c + 1] = jnp.sum(jnp.where(here, both, 0.0), 0, keepdims=True) * weight

        @pl.when(n != 4)
        def _():
            val_copy(n).start()

        return carry

    lax.fori_loop(0, 9, pick, 0)
    lnk_r[4] = lnk_s[4]
    val_r[4] = val_s[4]
    acc[...] = jnp.zeros_like(acc)

    def add(t, carry):
        n = lax.rem(t + 4, 9)

        @pl.when(n != 4)
        def _():
            lnk_copy(n).wait_recv()
            val_copy(n).wait_recv()

        target = lnk_r[n, 0:1]
        weight = lnk_r[n, 1:2].astype(F32).astype(BF16)
        col = (target & (CY - 1)).astype(F32).astype(BF16)
        row = (target >> 8).astype(F32).astype(BF16)
        index = wide(iota[...], CAP // 128)
        hot = jnp.where(index == col, one, none)
        here = index[:CX] == row
        high0, low0 = hi_lo(val_r[n, 0:1])
        high1, low1 = hi_lo(val_r[n, 1:2])
        spread = jnp.concatenate(
            [jnp.where(here, x, none) for x in (high0, high1, low0, low1, weight)], 0
        )
        acc[...] += lax.dot_general(
            spread, hot, (((1,), (1,)), ((), ())), preferred_element_type=F32
        )
        return carry

    lax.fori_loop(0, 9, add, 0)
    per = 1.0 / jnp.maximum(acc[4 * CX : 5 * CX], 1.0)
    rem[0] = (acc[0:CX] + acc[2 * CX : 3 * CX]) * per
    rem[1] = (acc[CX : 2 * CX] + acc[3 * CX : 4 * CX]) * per

    hand_over = pltpu.make_async_remote_copy(
        rem, hst, rs_sem, rr_sem, device_id=(1 - sec, tx, ty), device_id_type=MESH
    )

    def along_ty(d):
        return pltpu.make_async_remote_copy(
            red, red1.at[d], p1s_sem.at[d], p1r_sem.at[d],
            device_id=near(0, d), device_id_type=MESH,
        )

    def along_tx(d):
        return pltpu.make_async_remote_copy(
            red1.at[0], red2.at[d], p2s_sem.at[d], p2r_sem.at[d],
            device_id=(1 - sec, lax.rem(tx + d, 8), ty), device_id_type=MESH,
        )

    def folded(plane):
        total = plane[0:8]
        for g in range(1, 8):
            total = total + plane[8 * g : 8 * g + 8]
        return total[:, :128] + total[:, 128:]

    @pl.when(is_atm)
    def _():
        hand_over.start()
        red[0:8] = folded(out_flux[0, 0] - surface * rem[0])
        red[8:16] = folded(surface)
        for d in range(1, 8):
            along_ty(d).start()
        total = red[...]
        for d in range(1, 8):
            along_ty(d).wait_recv()
            total = total + red1[d]
        red1[0] = total
        for d in range(8):
            along_tx(d).start()
        for d in range(1, 8):
            along_ty(d).wait_send()
        for d in range(8):
            along_tx(d).wait_send()
        hand_over.wait_send()
        pltpu.make_async_copy(buf.at[1, :, pl.ds(TAB, CX)], out_state.at[0], out_sem).wait()

    @pl.when(is_ocn)
    def _():
        stress = (surface * rem[0], surface * rem[1])
        out_flux[0, 2] = stress[0]
        out_flux[0, 3] = stress[1]

        def levels(s, ch, start, stop, packed):
            slot = s
            first = ch * CH
            for g in range(8):
                part = slice(8 * g, 8 * g + 8)
                rows = slice(TAB + 8 * g, TAB + 8 * g + 8)
                c_up, c_down, c_left, c_right, c_mix = [cf[i, part] for i in range(5)]
                d_up, d_down, d_left, d_right = [cf[i, part] for i in range(6, 10)]
                own = lev[part].astype(F32)
                sx, sy = out_flux[0, 2, part], out_flux[0, 3, part]
                col_low, col_high = crecv[s, ch, 0, part], crecv[s, ch, 1, part]

                def level(kk, held):
                    before, value, pack0, pack1 = held
                    k = first + kk
                    depth_here = k.astype(F32)
                    following = buf[slot, k + 1, rows]
                    up, down, left, right = sides(slot, k, kk, g, value, col_low, col_high)
                    fade = jnp.broadcast_to(dec[pl.ds(k, 1), :], (8, 128))
                    flow = (
                        jnp.where(depth_here < d_up, c_up * (up - value), 0.0)
                        + jnp.where(depth_here < d_down, c_down * (down - value), 0.0)
                        + jnp.where(depth_here < d_left, c_left * (left - value), 0.0)
                        + jnp.where(depth_here < d_right, c_right * (right - value), 0.0)
                    )
                    flow = flow + c_mix * (
                        jnp.where(depth_here + 1.0 < own, following - value, 0.0) + (before - value)
                    )
                    flow = flow - wide(fade, 2) * (sx * (down - up) + sy * (right - left))
                    new = value + jnp.where(depth_here < own, flow, 0.0)
                    buf[1 - slot, k, rows] = new
                    if not packed:
                        return value, following, pack0, pack1
                    here = lane == kk
                    pack0 = jnp.where(here, pack_high(new, kk), pack0)
                    pack1 = jnp.where(here, pack_low(new, kk), pack1)
                    if g == 7:
                        rsend[1, ch, 0, pl.ds(kk, 1)] = new[7:8]
                    if g == 0:
                        rsend[1, ch, 1, pl.ds(kk, 1)] = new[0:1]
                    return value, following, pack0, pack1

                zero = jnp.zeros((8, 128), F32)
                held = (
                    buf[slot, jnp.maximum(first + start - 1, 0), rows],
                    buf[slot, first + start, rows],
                    zero,
                    zero,
                )
                held = lax.fori_loop(start, stop, level, held)
                if packed:
                    csend[1, ch, 0, part] = held[2]
                    csend[1, ch, 1, part] = held[3]

        def ocean_count(ch):
            return jnp.minimum(CH, OLEV - ch * CH)

        def halos_arrived_ocean(s, ch):
            for copy in halo_copies(s, ch):
                copy.wait_recv()

        for copy in halo_copies(0, 0):
            copy.wait_recv()
        static_part()
        for at, other in enumerate(shifted(depth, 1)):
            cf[6 + at] = other
        def deep_step(t, carry):
            ch = NCH - 1 - t
            halos_arrived_ocean(0, ch)
            return carry

        lax.fori_loop(0, NCH - 1, deep_step, 0)

        def step0(t, carry):
            ch = NCH - 1 - t
            rows_in(0, 0, ch, CH)
            levels(0, ch, 0, ocean_count(ch), True)
            for copy in halo_copies(1, ch):
                copy.start()
            return carry

        lax.fori_loop(0, NCH, step0, 0)

        gain = surface * 4.0 * c2
        hand_over.wait_recv()
        qb[...] = buf[1, 0, TAB : TAB + CX] + gain * (hst[0] + 0.3 * hst[1])
        q_moves = (
            (qb.at[CX - 8 : CX], qrow.at[0], near(1, 0)),
            (qb.at[0:8], qrow.at[1], near(-1, 0)),
            (qb.at[:, 128:256], qcol.at[0], near(0, 1)),
            (qb.at[:, 0:128], qcol.at[1], near(0, -1)),
        )
        q_copies = [
            pltpu.make_async_remote_copy(
                src, dst, qs_sem.at[i], qr_sem.at[i], device_id=there, device_id_type=MESH
            )
            for i, (src, dst, there) in enumerate(q_moves)
        ]
        for copy in q_copies:
            copy.start()

        def step1(t, carry):
            ch = NCH - 1 - t
            halos_arrived_ocean(1, ch)
            rows_in(1, 1, ch, CH)
            levels(1, ch, jnp.where(ch == 0, 2, 0), ocean_count(ch), False)
            return carry

        lax.fori_loop(0, NCH, step1, 0)
        deep = pltpu.make_async_copy(
            buf.at[0, pl.ds(2, LEV - 2), pl.ds(TAB, CX)], out_state.at[0, pl.ds(2, LEV - 2)], out_sem
        )
        deep.start()

        total = jnp.zeros((16, 128), F32)
        for d in range(8):
            along_tx(d).wait_recv()
            total = total + red2[d]
        fix = jnp.sum(total[0:8], keepdims=True) / jnp.maximum(jnp.sum(total[8:16], keepdims=True), 1.0)
        flux0 = surface * (hst[0] + fix)
        flux1 = surface * hst[1]
        out_flux[0, 0] = flux0
        out_flux[0, 1] = flux1
        buf[1, 0, TAB : TAB + CX] = qb[...] + gain * fix
        for copy in q_copies:
            copy.wait_recv()

        def gain_of(c2_edge, depth_edge):
            return (depth_edge > 0.0).astype(F32) * 4.0 * c2_edge

        for side, at, inner in ((0, TAB - 1, 7), (1, TAB + CX, 0)):
            edge = rrecv[0, 0, side]
            buf[1, 0, at : at + 1] = qrow[side, inner : inner + 1] + fix * gain_of(
                edge[CH + 2 : CH + 3], edge[CH + 1 : CH + 2]
            )
        low = gain_of(pltpu.roll(crecv[0, 0, 0], 128 - CH - 2, 1), pltpu.roll(crecv[0, 0, 0], 128 - CH - 1, 1))
        high = gain_of(pltpu.roll(crecv[0, 0, 1], 128 - CH - 2, 1), pltpu.roll(crecv[0, 0, 1], 128 - CH - 1, 1))
        lane_col = lax.broadcasted_iota(jnp.int32, (CX, 128), 1)
        crecv[1, 0, 0] = jnp.where(
            lane_col == 0, pltpu.roll(qcol[0], 1, 1) + fix * low, crecv[1, 0, 0]
        )
        crecv[1, 0, 1] = jnp.where(lane_col == 0, qcol[1] + fix * high, crecv[1, 0, 1])
        levels(1, 0, 0, 2, False)
        buf[0, 0, TAB : TAB + CX] = buf[0, 0, TAB : TAB + CX] + gain * (flux0 + 0.3 * flux1)
        shallow = pltpu.make_async_copy(
            buf.at[0, pl.ds(0, 2), pl.ds(TAB, CX)], out_state.at[0, pl.ds(0, 2)], in_sem.at[0]
        )
        shallow.start()
        for copy in q_copies:
            copy.wait_send()
        for ch in range(NCH):
            for copy in halo_copies(0, ch) + halo_copies(1, ch):
                copy.wait_send()
        deep.wait()
        shallow.wait()

    @pl.when(is_atm)
    def _():
        for s in range(3):
            for ch in range(NCH):
                for copy in halo_copies(s, ch):
                    copy.wait_send()

    for n in range(9):
        if n != 4:
            lnk_copy(n).wait_send()
            val_copy(n).wait_send()


def on_device(state, coeffs, forcing, levels, remap):
    vmem = pl.BlockSpec(memory_space=pltpu.VMEM)
    anywhere = pl.BlockSpec(memory_space=pl.ANY)
    dma = pltpu.SemaphoreType.DMA
    return pl.pallas_call(
        kernel,
        out_shape=(
            jax.ShapeDtypeStruct((1, LEV, CX, CY), F32),
            jax.ShapeDtypeStruct((1, 4, CX, CY), F32),
        ),
        in_specs=[anywhere, vmem, vmem, vmem, vmem],
        out_specs=(anywhere, vmem),
        scratch_shapes=[
            pltpu.VMEM((2, LEV, CX + 16, CY), F32),
            pltpu.VMEM((4, NCH, 2, 32, CY), F32),
            pltpu.VMEM((4, NCH, 2, CX, 128), F32),
            pltpu.VMEM((3, NCH, 2, 32, CY), F32),
            pltpu.VMEM((3, NCH, 2, CX, 128), F32),
            pltpu.VMEM((10, CX, CY), F32),
            pltpu.VMEM((9, 2, CAP), jnp.int32),
            pltpu.VMEM((9, 2, CAP), jnp.int32),
            pltpu.VMEM((9, 2, CAP), F32),
            pltpu.VMEM((9, 2, CAP), F32),
            pltpu.VMEM((5 * CX, CY), F32),
            pltpu.VMEM((4 * CX, CY), BF16),
            pltpu.VMEM((CY, 128), BF16),
            pltpu.VMEM((LEV, 128), F32),
            pltpu.VMEM((2, CX, CY), F32),
            pltpu.VMEM((2, CX, CY), F32),
            pltpu.VMEM((CX, CY), F32),
            pltpu.VMEM((2, 8, CY), F32),
            pltpu.VMEM((2, CX, 128), F32),
            pltpu.VMEM((16, 128), F32),
            pltpu.VMEM((8, 16, 128), F32),
            pltpu.VMEM((8, 16, 128), F32),
            dma((NCH,)),
            dma,
            dma((3, NCH, 4)),
            dma((3, NCH, 4)),
            dma((9,)),
            dma((9,)),
            dma((9,)),
            dma((9,)),
            dma,
            dma,
            dma((4,)),
            dma((4,)),
            dma((8,)),
            dma((8,)),
            dma((8,)),
            dma((8,)),
        ],
        compiler_params=pltpu.CompilerParams(
            collective_id=0, has_side_effects=True, vmem_limit_bytes=60 << 20
        ),
        name="window",
    )(state, coeffs, forcing, levels, remap)


def solution(mesh):
    return jax.shard_map(
        on_device,
        mesh=mesh,
        in_specs=(
            P("sec", None, "tx", "ty"),
            P("sec", None, "tx", "ty"),
            P(None, "tx", "ty"),
            P("tx", "ty"),
            P(None, ("tx", "ty")),
        ),
        out_specs=(P("sec", None, "tx", "ty"), P("sec", None, "tx", "ty")),
        check_vma=False,
    )
```

time: 461 us -> 193 us (0.42)
  the two profiles are of different devices: /device:TPU:0 before, /device:TPU:1 now
where the time goes in v1:
time: 193 us; the launch traced here: 192 us
  Pallas kernels  186 us (96%)
  local copies, waits for them, and re-layouts  5.85 us (3%)
    pallas_call x1, Pallas kernels, on_device(): pl.pallas_call(kernel, out_shape=(jax.ShapeDtypeStruct((1, LEV, CX, CY),...  186 us
    unnamed x4, local copies, waits for them, and re-layouts  5.85 us

profile of v1, /device:TPU:1, one launch (start us, length us, event | category | flops | bytes accessed | tf_op | source)
XLA Modules:
  0.0 192.4 jit_solution(16071530948388619654)
XLA Ops:
  0.6 185.9 %window.1 = (f32[1,72,64,256]{3,2,1,0:T(8,128)}, f32[1,4,64,256]{3,2,1,0:T(8,128)}) custom-call(f32[1,72,64,256]{3,2,1,0:T(8,128)} %state.1, f32[1,3,64,256]{3,2,1,0:T(8,128)} %coef.1, f32[4,64,256]{2,1,0:T(8,128)} %forc.1, s32[64,256]{1,0:T(8,128)} %lev.1, s32[5,36864]{1,0:T(8,128)} %remap.1), custom_call_target="tpu_custom_call" | custom-call | tf_op jit(solution)/shard_map/window/pallas_call | solution.py:560
  186.6 0.0 copy-start
  186.6 5.1 %copy.9 = f32[1,72,64,256]{3,2,1,0:T(8,128)} copy(f32[1,72,64,256]{3,2,1,0:T(8,128)} %get-tuple-element.4) | data formatting | bytes 9437184
  191.7 0.0 copy-done
  191.7 0.7 copy.10
Async XLA Ops:
  186.6 5.2 %copy-start = (f32[1,4,64,256]{3,2,1,0:T(8,128)S(1)}, f32[1,4,64,256]{3,2,1,0:T(8,128)}, u32[]{:S(2)}) copy-start(f32[1,4,64,256]{3,2,1,0:T(8,128)} %get-tuple-element.5) | copy-start | bytes 786436

commit v2 on v1

v2 whole, which is shorter than its diff:
```python
import jax
import jax.numpy as jnp
from jax import lax
from jax.experimental import pallas as pl
from jax.experimental.pallas import tpu as pltpu
from jax.sharding import PartitionSpec as P

LEV, OLEV, CX, CY = 72, 60, 64, 256
CAP = 4096
TAB = 8
CH = 24
NCH = LEV // CH
STACK = 8
F32, BF16 = jnp.float32, jnp.bfloat16
MESH = pl.DeviceIdType.MESH


def hi_lo(x):
    high = x.astype(BF16)
    return high, (x - high.astype(F32)).astype(BF16)


def wide(x, count):
    return jnp.concatenate([x] * count, 1)


def kernel(
    state, coef, forc, lev, remap, out_state, out_flux,
    buf_a, buf_b, top, top2, rsend, csend, rrecv, crecv, ccomb, cf, lnk_s, lnk_r, val_s, val_r, acc, fb, iota,
    dec, rem, hst, qb, qrow, qcol, red, red1, red2,
    in_sem, out_sem, hs_sem, hr_sem, ls_sem, lr_sem, vs_sem, vr_sem, rs_sem, rr_sem,
    qs_sem, qr_sem, p1s_sem, p1r_sem, p2s_sem, p2r_sem,
):
    sec, tx, ty = lax.axis_index("sec"), lax.axis_index("tx"), lax.axis_index("ty")
    is_atm = sec == 0
    is_ocn = sec == 1

    def near(dx, dy):
        return (sec, lax.rem(tx + dx + 8, 8), lax.rem(ty + dy + 8, 8))

    barrier = pltpu.get_barrier_semaphore()
    for dx in (-1, 0, 1, 4):
        for dy in (-1, 0, 1):
            if dx != 0 or dy != 0:
                pl.semaphore_signal(barrier, 1, device_id=near(dx, dy), device_id_type=MESH)
    for dy in range(2, 7):
        pl.semaphore_signal(barrier, 1, device_id=near(0, dy), device_id_type=MESH)
    for dx in range(8):
        pl.semaphore_signal(
            barrier, 1, device_id=(1 - sec, lax.rem(tx + dx, 8), ty), device_id_type=MESH
        )

    def state_in(ch):
        return pltpu.make_async_copy(
            state.at[0, pl.ds(ch * CH, CH)],
            buf_a.at[pl.ds(ch * CH, CH), pl.ds(TAB, CX)],
            in_sem.at[ch],
        )

    for ch in range(NCH):
        state_in(ch).start()

    kap, mix, c2 = coef[0, 0], coef[0, 1], coef[0, 2]
    depth = jnp.where(is_atm, jnp.full((CX, CY), float(LEV), F32), lev[...].astype(F32))
    surface = (lev[...] > 0).astype(F32)

    def target_of(n):
        row_step = n // 3
        return near(row_step - 1 + 3 * (row_step // 2), n % 3 - 1)

    def lnk_copy(n):
        return pltpu.make_async_remote_copy(
            lnk_s.at[n], lnk_r.at[n], ls_sem.at[n], lr_sem.at[n],
            device_id=target_of(n), device_id_type=MESH,
        )

    def val_copy(n):
        return pltpu.make_async_remote_copy(
            val_s.at[n], val_r.at[n], vs_sem.at[n], vr_sem.at[n],
            device_id=target_of(n), device_id_type=MESH,
        )

    def halo_copies(s, ch):
        out = []
        for d, (there, low) in enumerate(
            ((near(1, 0), 0), (near(-1, 0), 1), (near(0, 1), 0), (near(0, -1), 1))
        ):
            source = rsend.at[s, ch, low] if d < 2 else csend.at[s, ch]
            recv = rrecv if d < 2 else crecv
            out.append(
                pltpu.make_async_remote_copy(
                    source, recv.at[s, ch, low], hs_sem.at[s, ch, d], hr_sem.at[s, ch, d],
                    device_id=there, device_id_type=MESH,
                )
            )
        return out

    def edge_copies():
        moves = (
            (qb.at[CX - 8 : CX], qrow.at[0], near(1, 0)),
            (qb.at[0:8], qrow.at[1], near(-1, 0)),
            (qb.at[:, 128:256], qcol.at[0], near(0, 1)),
            (qb.at[:, 0:128], qcol.at[1], near(0, -1)),
        )
        return [
            pltpu.make_async_remote_copy(
                source, there, qs_sem.at[i], qr_sem.at[i], device_id=device, device_id_type=MESH
            )
            for i, (source, there, device) in enumerate(moves)
        ]

    lane = lax.broadcasted_iota(jnp.int32, (8, 128), 1)
    lane3 = lax.broadcasted_iota(jnp.int32, (1, 8, 128), 2)
    lane_col = lax.broadcasted_iota(jnp.int32, (CX, 128), 1)

    def pack_edges(src, s, ch, extras=()):
        for g in range(8):
            packed = jnp.zeros((8, 128), F32)
            for i in range(CH + len(extras)):
                if i < CH:
                    both = src[ch * CH + i, TAB + 8 * g : TAB + 8 * g + 8]
                else:
                    both = extras[i - CH][8 * g : 8 * g + 8]
                ends = jnp.where(lane < 64, both[:, :128], both[:, 128:])
                packed = jnp.where((lane >> 1) == i, pltpu.roll(ends, 2 * i + 1, 1), packed)
            csend[s, ch, 8 * g : 8 * g + 8] = packed
        for i in range(0, CH, 8):
            rsend[s, ch, 0, i : i + 8] = src[pl.ds(ch * CH + i, 8), TAB + CX - 1]
            rsend[s, ch, 1, i : i + 8] = src[pl.ds(ch * CH + i, 8), TAB]
        for copy in halo_copies(s, ch):
            copy.start()

    def unpack_edges(src, s, ch):
        before, after = pltpu.roll(crecv[s, ch, 0], 1, 1), pltpu.roll(crecv[s, ch, 1], 127, 1)
        ccomb[...] = jnp.where((lane_col & 1) == 1, before, after)
        src[pl.ds(ch * CH, CH), TAB - 1] = rrecv[s, ch, 0, 0:CH]
        src[pl.ds(ch * CH, CH), TAB + CX] = rrecv[s, ch, 1, 0:CH]

    def halo_wait(s, ch):
        for copy in halo_copies(s, ch):
            copy.wait_recv()

    def sides(value, ends):
        first, last = value[:, :, :128], value[:, :, 128:]
        right_a, right_b = pltpu.roll(first, 1, 2), pltpu.roll(last, 1, 2)
        left_a, left_b = pltpu.roll(first, 127, 2), pltpu.roll(last, 127, 2)
        left = jnp.concatenate(
            [jnp.where(lane3 == 0, ends, right_a), jnp.where(lane3 == 0, right_a, right_b)], 2
        )
        right = jnp.concatenate(
            [jnp.where(lane3 == 127, left_b, left_a), jnp.where(lane3 == 127, ends, left_b)], 2
        )
        return left, right

    def ends_of(part, i, count):
        columns = ccomb[part]
        return jnp.concatenate(
            [pltpu.roll(columns, lax.rem(255 - 2 * (i + j), 128), 1)[None] for j in range(count)], 0
        )

    def atm_batch(src, dst, k, count, ends, g):
        part, at = slice(8 * g, 8 * g + 8), TAB + 8 * g
        c_up, c_down, c_left, c_right, c_mix, c_own = [cf[i, part][None] for i in range(6)]
        value = src[pl.ds(k, count), at : at + 8]
        before = src[pl.ds(jnp.maximum(k - 1, 0), 1), at : at + 8]
        after = src[pl.ds(jnp.minimum(k + count, LEV - 1), 1), at : at + 8]
        if count > 1:
            before = jnp.concatenate([before, value[:-1]], 0)
            after = jnp.concatenate([value[1:], after], 0)
        up = src[pl.ds(k, count), at - 1 : at + 7]
        down = src[pl.ds(k, count), at + 1 : at + 9]
        left, right = sides(value, ends)
        new = c_own * value + c_mix * (before + after)
        dst[pl.ds(k, count), at : at + 8] = (
            new + (c_up * up + c_down * down) + (c_left * left + c_right * right)
        )

    def cool(src, dst):
        rows = slice(TAB, TAB + CX)
        dst[0, rows] = dst[0, rows] - coef[0, 2] * (src[0, rows] - forc[3])

    def atm_chunk(src, dst, s, ch, wait=True):
        if wait:
            halo_wait(s, ch)
        unpack_edges(src, s, ch)

        def batch(b, carry):
            for g in range(8):
                ends = ends_of(slice(8 * g, 8 * g + 8), b * STACK, STACK)
                atm_batch(src, dst, ch * CH + b * STACK, STACK, ends, g)
            return carry

        lax.fori_loop(0, CH // STACK, batch, 0)
        if isinstance(ch, int):
            if ch == 0:
                cool(src, dst)
        else:
            pl.when(ch == 0)(lambda: cool(src, dst))
        if s < 2:
            pack_edges(dst, s + 1, ch)

    lane_all = lax.broadcasted_iota(jnp.int32, (CX, CY), 1)

    def around(plane, at):
        low_row = rrecv[0, 0, 0, CH + at : CH + at + 1]
        high_row = rrecv[0, 0, 1, CH + at : CH + at + 1]
        low_col = crecv[0, 0, 0][:, 2 * (CH + at) : 2 * (CH + at) + 1]
        high_col = crecv[0, 0, 1][:, 2 * (CH + at) + 1 : 2 * (CH + at) + 2]
        return (
            jnp.concatenate([low_row, plane[:-1]], 0),
            jnp.concatenate([plane[1:], high_row], 0),
            jnp.where(lane_all == 0, low_col, pltpu.roll(plane, 1, 1)),
            jnp.where(lane_all == CY - 1, high_col, pltpu.roll(plane, CY - 1, 1)),
        )

    def coefficients():
        total = jnp.zeros((CX, CY), F32)
        for at, other in enumerate(around(kap, 0)):
            half = 0.5 * (kap + other)
            cf[at] = half
            total = total + half
        cf[4] = mix
        cf[5] = (1.0 - total) - 2.0 * mix
        for at, other in enumerate(around(depth, 1)):
            cf[6 + at] = other

    pl.semaphore_wait(barrier, 24)
    for side, row in ((0, CX - 1), (1, 0)):
        rsend[0, 0, side, CH : CH + 8] = jnp.zeros((8, CY), F32)
        for at, plane in enumerate((kap, depth, c2)):
            rsend[0, 0, side, CH + at : CH + at + 1] = plane[row : row + 1]
    state_in(0).wait()
    pack_edges(buf_a, 0, 0, (kap, depth, c2))

    def more(ch, carry):
        state_in(ch).wait()
        pack_edges(buf_a, 0, ch)
        return carry

    lax.fori_loop(1, NCH, more, 0)
    for n in range(9):
        lnk_s[n] = remap[3:5, n * CAP : (n + 1) * CAP]
        if n != 4:
            lnk_copy(n).start()
    iota[...] = lax.broadcasted_iota(jnp.int32, (CY, 128), 0).astype(F32).astype(BF16)

    speed = 0.2 * jnp.sqrt(1.0 + forc[0] * forc[0] + forc[1] * forc[1])

    @pl.when(is_atm)
    def _():
        halo_wait(0, 0)
        coefficients()
        atm_chunk(buf_a, buf_b, 0, 0, False)
        atm_chunk(buf_a, buf_b, 0, 1)
        halo_wait(1, 0)
        unpack_edges(buf_b, 1, 0)
        for g in range(8):
            part = slice(8 * g, 8 * g + 8)
            atm_batch(buf_b, top, 0, 2, ends_of(part, 0, 2), g)
        cool(buf_b, top)
        qb[...] = top[0, TAB : TAB + CX]
        for copy in edge_copies():
            copy.start()
        atm_chunk(buf_a, buf_b, 0, 2)
        for copy in edge_copies():
            copy.wait_recv()
        top[0, TAB - 1 : TAB] = qrow[0, 7:8]
        top[0, TAB + CX : TAB + CX + 1] = qrow[1, 0:1]
        for g in range(8):
            part = slice(8 * g, 8 * g + 8)
            ends = jnp.where(lane == 0, pltpu.roll(qcol[0, part], 1, 1), pltpu.roll(qcol[1, part], 127, 1))
            atm_batch(top, top2, 0, 1, ends[None], g)
        cool(top, top2)
        heat = c2 * (top2[0, TAB : TAB + CX] - forc[3])
        out_flux[0, 0] = heat
        out_flux[0, 1] = forc[2] - 0.5 * heat
        out_flux[0, 2] = speed * forc[0]
        out_flux[0, 3] = speed * forc[1]

    @pl.when(is_ocn)
    def _():
        out_flux[0, 0] = speed * forc[0]
        out_flux[0, 1] = speed * forc[1]

    for c in range(2):
        high, low = hi_lo(out_flux[0, c])
        fb[CX * c : CX * (c + 1)] = high
        fb[2 * CX + CX * c : 2 * CX + CX * (c + 1)] = low
    one, none = jnp.array(1, BF16), jnp.array(0, BF16)

    def pick(t, carry):
        n = lax.rem(t + 5, 9)
        at = pl.multiple_of(n * CAP, CAP)
        source = remap[0:1, pl.ds(at, CAP)]
        weight = remap[4:5, pl.ds(at, CAP)].astype(F32)
        col = (source & (CY - 1)).astype(F32).astype(BF16)
        hot = jnp.where(wide(iota[...], CAP // 128) == col, one, none)
        product = jnp.dot(fb[...], hot, preferred_element_type=F32)
        here = lax.broadcasted_iota(jnp.int32, (CX, CAP), 0) == (source >> 8)
        for c in range(2):
            both = product[CX * c : CX * (c + 1)] + product[2 * CX + CX * c : 2 * CX + CX * (c + 1)]
            val_s[n, c : c + 1] = jnp.sum(jnp.where(here, both, 0.0), 0, keepdims=True) * weight

        @pl.when(n != 4)
        def _():
            val_copy(n).start()

        return carry

    lax.fori_loop(0, 9, pick, 0)
    lnk_r[4] = lnk_s[4]
    val_r[4] = val_s[4]
    acc[...] = jnp.zeros_like(acc)

    def add(t, carry):
        n = lax.rem(t + 4, 9)

        @pl.when(n != 4)
        def _():
            lnk_copy(n).wait_recv()
            val_copy(n).wait_recv()

        target = lnk_r[n, 0:1]
        weight = lnk_r[n, 1:2].astype(F32).astype(BF16)
        col = (target & (CY - 1)).astype(F32).astype(BF16)
        row = (target >> 8).astype(F32).astype(BF16)
        index = wide(iota[...], CAP // 128)
        hot = jnp.where(index == col, one, none)
        here = index[:CX] == row
        high0, low0 = hi_lo(val_r[n, 0:1])
        high1, low1 = hi_lo(val_r[n, 1:2])
        spread = jnp.concatenate(
            [jnp.where(here, x, none) for x in (high0, high1, low0, low1, weight)], 0
        )
        acc[...] += lax.dot_general(
            spread, hot, (((1,), (1,)), ((), ())), preferred_element_type=F32
        )
        return carry

    lax.fori_loop(0, 9, add, 0)
    per = 1.0 / jnp.maximum(acc[4 * CX : 5 * CX], 1.0)
    rem[0] = (acc[0:CX] + acc[2 * CX : 3 * CX]) * per
    rem[1] = (acc[CX : 2 * CX] + acc[3 * CX : 4 * CX]) * per

    hand_over = pltpu.make_async_remote_copy(
        rem, hst, rs_sem, rr_sem, device_id=(1 - sec, tx, ty), device_id_type=MESH
    )

    def along_ty(d):
        return pltpu.make_async_remote_copy(
            red, red1.at[d], p1s_sem.at[d], p1r_sem.at[d],
            device_id=near(0, d), device_id_type=MESH,
        )

    def along_tx(d):
        return pltpu.make_async_remote_copy(
            red1.at[0], red2.at[d], p2s_sem.at[d], p2r_sem.at[d],
            device_id=(1 - sec, lax.rem(tx + d, 8), ty), device_id_type=MESH,
        )

    def folded(plane):
        total = plane[0:8]
        for g in range(1, 8):
            total = total + plane[8 * g : 8 * g + 8]
        return total[:, :128] + total[:, 128:]

    def state_out(src, ch):
        return pltpu.make_async_copy(
            src.at[pl.ds(ch * CH, CH), pl.ds(TAB, CX)],
            out_state.at[0, pl.ds(ch * CH, CH)],
            out_sem.at[ch],
        )

    @pl.when(is_atm)
    def _():
        hand_over.start()
        red[0:8] = folded(out_flux[0, 0] - surface * rem[0])
        red[8:16] = folded(surface)
        for d in range(1, 8):
            along_ty(d).start()
        atm_chunk(buf_b, buf_a, 1, 0, False)
        total = red[...]
        for d in range(1, 8):
            along_ty(d).wait_recv()
            total = total + red1[d]
        red1[0] = total
        for d in range(8):
            along_tx(d).start()

        def second(ch, carry):
            atm_chunk(buf_b, buf_a, 1, ch)
            return carry

        lax.fori_loop(1, NCH, second, 0)

        def third(ch, carry):
            atm_chunk(buf_a, buf_b, 2, ch)
            state_out(buf_b, ch).start()
            return carry

        lax.fori_loop(0, NCH, third, 0)
        for d in range(1, 8):
            along_ty(d).wait_send()
        for d in range(8):
            along_tx(d).wait_send()
        hand_over.wait_send()
        for s in range(3):
            for ch in range(NCH):
                for copy in halo_copies(s, ch):
                    copy.wait_send()
        for ch in range(NCH):
            state_out(buf_b, ch).wait()

    @pl.when(is_ocn)
    def _():
        out_flux[0, 2] = surface * rem[0]
        out_flux[0, 3] = surface * rem[1]
        level8 = lax.broadcasted_iota(jnp.int32, (LEV, 8, 128), 0).astype(F32)
        dec[...] = 0.5 * jnp.exp(level8 * (-1 / 8))
        halo_wait(0, 0)
        coefficients()

        def ocn_batch(src, dst, k, count, ends, g):
            part, at = slice(8 * g, 8 * g + 8), TAB + 8 * g
            c_up, c_down, c_left, c_right, c_mix = [cf[i, part][None] for i in range(5)]
            d_up, d_down, d_left, d_right = [cf[i, part][None] for i in range(6, 10)]
            own = lev[part].astype(F32)[None]
            sx, sy = out_flux[0, 2, part][None], out_flux[0, 3, part][None]
            here = (lax.broadcasted_iota(jnp.int32, (count, 8, CY), 0) + k).astype(F32)
            fade = dec[pl.ds(k, count)]
            value = src[pl.ds(k, count), at : at + 8]
            before = src[pl.ds(jnp.maximum(k - 1, 0), 1), at : at + 8]
            after = src[pl.ds(k + count, 1), at : at + 8]
            before = jnp.concatenate([before, value[:-1]], 0)
            after = jnp.concatenate([value[1:], after], 0)
            up = src[pl.ds(k, count), at - 1 : at + 7]
            down = src[pl.ds(k, count), at + 1 : at + 9]
            left, right = sides(value, ends)
            flow = (
                jnp.where(here < d_up, c_up * (up - value), 0.0)
                + jnp.where(here < d_down, c_down * (down - value), 0.0)
                + jnp.where(here < d_left, c_left * (left - value), 0.0)
                + jnp.where(here < d_right, c_right * (right - value), 0.0)
            )
            flow = flow + c_mix * (
                jnp.where(here + 1.0 < own, after - value, 0.0) + (before - value)
            )
            flow = flow - jnp.concatenate([fade, fade], 2) * (sx * (down - up) + sy * (right - left))
            dst[pl.ds(k, count), at : at + 8] = value + jnp.where(here < own, flow, 0.0)

        def ocn_chunk(src, dst, s, ch):
            unpack_edges(src, s, ch)

            def batch(b, carry):
                for g in range(8):
                    ends = ends_of(slice(8 * g, 8 * g + 8), b * STACK, STACK)
                    ocn_batch(src, dst, ch * CH + b * STACK, STACK, ends, g)
                return carry

            batches = jnp.minimum(CH, OLEV - ch * CH + STACK - 1) // STACK
            lax.fori_loop(0, batches, batch, 0)

        def first(ch, carry):
            @pl.when(ch > 0)
            def _():
                halo_wait(0, ch)

            ocn_chunk(buf_a, buf_b, 0, ch)
            pack_edges(buf_b, 1, ch)
            return carry

        lax.fori_loop(0, NCH, first, 0)

        def second(ch, carry):
            halo_wait(1, ch)
            ocn_chunk(buf_b, buf_a, 1, ch)

            @pl.when(ch > 0)
            def _():
                state_out(buf_a, ch).start()

            return carry

        lax.fori_loop(0, NCH, second, 0)
        deep = pltpu.make_async_copy(
            buf_a.at[pl.ds(2, CH - 2), pl.ds(TAB, CX)], out_state.at[0, pl.ds(2, CH - 2)], out_sem.at[0]
        )
        deep.start()

        gain = surface * 4.0 * c2
        hand_over.wait_recv()
        qb[...] = buf_b[0, TAB : TAB + CX] + gain * (hst[0] + 0.3 * hst[1])
        for copy in edge_copies():
            copy.start()

        total = jnp.zeros((16, 128), F32)
        for d in range(8):
            along_tx(d).wait_recv()
            total = total + red2[d]
        fix = jnp.sum(total[0:8], keepdims=True) / jnp.maximum(jnp.sum(total[8:16], keepdims=True), 1.0)
        flux0 = surface * (hst[0] + fix)
        flux1 = surface * hst[1]
        out_flux[0, 0] = flux0
        out_flux[0, 1] = flux1
        buf_b[0, TAB : TAB + CX] = qb[...] + gain * fix
        for copy in edge_copies():
            copy.wait_recv()

        def gain_of(c2_edge, depth_edge):
            return (depth_edge > 0.0).astype(F32) * 4.0 * c2_edge

        for side, at, inner in ((0, TAB - 1, 7), (1, TAB + CX, 0)):
            edge = rrecv[0, 0, side]
            buf_b[0, at : at + 1] = qrow[side, inner : inner + 1] + fix * gain_of(
                edge[CH + 2 : CH + 3], edge[CH + 1 : CH + 2]
            )
        lane_c2, lane_depth = 2 * (CH + 2), 2 * (CH + 1)
        low = gain_of(
            pltpu.roll(crecv[0, 0, 0], 128 - lane_c2, 1), pltpu.roll(crecv[0, 0, 0], 128 - lane_depth, 1)
        )
        high = gain_of(
            pltpu.roll(crecv[0, 0, 1], 126 - lane_c2, 1), pltpu.roll(crecv[0, 0, 1], 126 - lane_depth, 1)
        )
        surface_ends = jnp.where(
            lane_col == 0,
            pltpu.roll(qcol[0], 1, 1) + fix * low,
            pltpu.roll(qcol[1], 127, 1) + fix * high,
        )
        unpack_columns = pltpu.roll(crecv[1, 0, 0], 1, 1), pltpu.roll(crecv[1, 0, 1], 127, 1)
        ccomb[...] = jnp.where((lane_col & 1) == 1, unpack_columns[0], unpack_columns[1])
        for g in range(8):
            part = slice(8 * g, 8 * g + 8)
            ends = jnp.concatenate([surface_ends[part][None], ends_of(part, 1, 1)], 0)
            ocn_batch(buf_b, buf_a, 0, 2, ends, g)
        buf_a[0, TAB : TAB + CX] = buf_a[0, TAB : TAB + CX] + gain * (flux0 + 0.3 * flux1)
        shallow = pltpu.make_async_copy(
            buf_a.at[pl.ds(0, 2), pl.ds(TAB, CX)], out_state.at[0, pl.ds(0, 2)], in_sem.at[0]
        )
        shallow.start()
        for s in range(2):
            for ch in range(NCH):
                for copy in halo_copies(s, ch):
                    copy.wait_send()
        deep.wait()
        for ch in range(1, NCH):
            state_out(buf_a, ch).wait()
        shallow.wait()

    for copy in edge_copies():
        copy.wait_send()
    for n in range(9):
        if n != 4:
            lnk_copy(n).wait_send()
            val_copy(n).wait_send()


def on_device(state, coeffs, forcing, levels, remap):
    vmem = pl.BlockSpec(memory_space=pltpu.VMEM)
    anywhere = pl.BlockSpec(memory_space=pl.ANY)
    dma = pltpu.SemaphoreType.DMA
    return pl.pallas_call(
        kernel,
        out_shape=(
            jax.ShapeDtypeStruct((1, LEV, CX, CY), F32),
            jax.ShapeDtypeStruct((1, 4, CX, CY), F32),
        ),
        in_specs=[anywhere, vmem, vmem, vmem, vmem],
        out_specs=(anywhere, vmem),
        scratch_shapes=[
            pltpu.VMEM((LEV, CX + 16, CY), F32),
            pltpu.VMEM((LEV, CX + 16, CY), F32),
            pltpu.VMEM((2, CX + 16, CY), F32),
            pltpu.VMEM((2, CX + 16, CY), F32),
            pltpu.VMEM((3, NCH, 2, 32, CY), F32),
            pltpu.VMEM((3, NCH, CX, 128), F32),
            pltpu.VMEM((3, NCH, 2, 32, CY), F32),
            pltpu.VMEM((3, NCH, 2, CX, 128), F32),
            pltpu.VMEM((CX, 128), F32),
            pltpu.VMEM((10, CX, CY), F32),
            pltpu.VMEM((9, 2, CAP), jnp.int32),
            pltpu.VMEM((9, 2, CAP), jnp.int32),
            pltpu.VMEM((9, 2, CAP), F32),
            pltpu.VMEM((9, 2, CAP), F32),
            pltpu.VMEM((5 * CX, CY), F32),
            pltpu.VMEM((4 * CX, CY), BF16),
            pltpu.VMEM((CY, 128), BF16),
            pltpu.VMEM((LEV, 8, 128), F32),
            pltpu.VMEM((2, CX, CY), F32),
            pltpu.VMEM((2, CX, CY), F32),
            pltpu.VMEM((CX, CY), F32),
            pltpu.VMEM((2, 8, CY), F32),
            pltpu.VMEM((2, CX, 128), F32),
            pltpu.VMEM((16, 128), F32),
            pltpu.VMEM((8, 16, 128), F32),
            pltpu.VMEM((8, 16, 128), F32),
            dma((NCH,)),
            dma((NCH,)),
            dma((3, NCH, 4)),
            dma((3, NCH, 4)),
            dma((9,)),
            dma((9,)),
            dma((9,)),
            dma((9,)),
            dma,
            dma,
            dma((4,)),
            dma((4,)),
            dma((8,)),
            dma((8,)),
            dma((8,)),
            dma((8,)),
        ],
        compiler_params=pltpu.CompilerParams(
            collective_id=0, has_side_effects=True, vmem_limit_bytes=60 << 20
        ),
        name="window",
    )(state, coeffs, forcing, levels, remap)


def solution(mesh):
    return jax.shard_map(
        on_device,
        mesh=mesh,
        in_specs=(
            P("sec", None, "tx", "ty"),
            P("sec", None, "tx", "ty"),
            P(None, "tx", "ty"),
            P("tx", "ty"),
            P(None, ("tx", "ty")),
        ),
        out_specs=(P("sec", None, "tx", "ty"), P("sec", None, "tx", "ty")),
        check_vma=False,
    )
```

time: 193 us -> 71.9 us (0.37)
  the two profiles are of different devices: /device:TPU:1 before, /device:TPU:0 now
where the time goes in v2:
time: 71.9 us; the launch traced here: 71.6 us
  Pallas kernels  65.1 us (91%)
  local copies, waits for them, and re-layouts  5.85 us (8%)
    pallas_call x1, Pallas kernels, on_device(): pl.pallas_call(kernel, out_shape=(jax.ShapeDtypeStruct((1, LEV, CX, CY),...  65.1 us
    unnamed x4, local copies, waits for them, and re-layouts  5.85 us

profile of v2, /device:TPU:0, one launch (start us, length us, event | category | flops | bytes accessed | tf_op | source)
XLA Modules:
  0.0 71.6 jit_solution(13702093577889807112)
XLA Ops:
  0.6 65.1 %window.1 = (f32[1,72,64,256]{3,2,1,0:T(8,128)}, f32[1,4,64,256]{3,2,1,0:T(8,128)}) custom-call(f32[1,72,64,256]{3,2,1,0:T(8,128)} %state.1, f32[1,3,64,256]{3,2,1,0:T(8,128)} %coef.1, f32[4,64,256]{2,1,0:T(8,128)} %forc.1, s32[64,256]{1,0:T(8,128)} %lev.1, s32[5,36864]{1,0:T(8,128)} %remap.1), custom_call_target="tpu_custom_call" | custom-call | tf_op jit(solution)/shard_map/window/pallas_call | solution.py:561
  65.7 0.0 copy-start
  65.7 5.1 %copy.9 = f32[1,72,64,256]{3,2,1,0:T(8,128)} copy(f32[1,72,64,256]{3,2,1,0:T(8,128)} %get-tuple-element.4) | data formatting | bytes 9437184
  70.9 0.0 copy-done
  70.9 0.7 copy.10
Async XLA Ops:
  65.7 5.2 %copy-start = (f32[1,4,64,256]{3,2,1,0:T(8,128)S(1)}, f32[1,4,64,256]{3,2,1,0:T(8,128)}, u32[]{:S(2)}) copy-start(f32[1,4,64,256]{3,2,1,0:T(8,128)} %get-tuple-element.5) | copy-start | bytes 786436

commit v3 on v2

--- a/solution.py
+++ b/solution.py
@@ -25,10 +25,10 @@
 
 
 def kernel(
-    state, coef, forc, lev, remap, out_state, out_flux,
-    buf_a, buf_b, top, top2, rsend, csend, rrecv, crecv, ccomb, cf, lnk_s, lnk_r, val_s, val_r, acc, fb, iota,
-    dec, rem, hst, qb, qrow, qcol, red, red1, red2,
-    in_sem, out_sem, hs_sem, hr_sem, ls_sem, lr_sem, vs_sem, vr_sem, rs_sem, rr_sem,
+    state, coef_in, forc_in, lev_in, remap_in, out_state, out_flux,
+    coef, forc, lev, remap, buf_a, buf_b, top, top2, rsend, csend, rrecv, crecv, ccomb, cf, lnk_s, lnk_r, val_s, val_r, acc, fb, iota,
+    dec, rem, hst, per, qb, qcs, qrow, qcol, red, red1, red2,
+    in_sem, hs_sem, hr_sem, ls_sem, lr_sem, fs_sem, fr_sem, ps_sem, pr_sem, vs_sem, vr_sem, rs_sem, rr_sem,
     qs_sem, qr_sem, p1s_sem, p1r_sem, p2s_sem, p2r_sem,
 ):
     sec, tx, ty = lax.axis_index("sec"), lax.axis_index("tx"), lax.axis_index("ty")
@@ -57,8 +57,21 @@
             in_sem.at[ch],
         )
 
-    for ch in range(NCH):
+    small_in = [
+        pltpu.make_async_copy(source, there, in_sem.at[NCH + i])
+        for i, (source, there) in enumerate(
+            ((coef_in, coef), (lev_in, lev), (forc_in, forc), (remap_in, remap))
+        )
+    ]
+    for copy in small_in[:3]:
+        copy.start()
+    state_in(0).start()
+    small_in[3].start()
+    for ch in range(1, NCH):
         state_in(ch).start()
+    iota[...] = lax.broadcasted_iota(jnp.int32, (CY, 128), 0).astype(F32).astype(BF16)
+    for copy in small_in[:3]:
+        copy.wait()
 
     kap, mix, c2 = coef[0, 0], coef[0, 1], coef[0, 2]
     depth = jnp.where(is_atm, jnp.full((CX, CY), float(LEV), F32), lev[...].astype(F32))
@@ -72,6 +85,12 @@
         return pltpu.make_async_remote_copy(
             lnk_s.at[n], lnk_r.at[n], ls_sem.at[n], lr_sem.at[n],
             device_id=target_of(n), device_id_type=MESH,
+        )
+
+    def lnk_pass(n):
+        return pltpu.make_async_remote_copy(
+            lnk_r.at[n], lnk_r.at[n], fs_sem.at[n], fr_sem.at[n],
+            device_id=(1 - sec, tx, ty), device_id_type=MESH,
         )
 
     def val_copy(n):
@@ -85,11 +104,15 @@
         for d, (there, low) in enumerate(
             ((near(1, 0), 0), (near(-1, 0), 1), (near(0, 1), 0), (near(0, -1), 1))
         ):
-            source = rsend.at[s, ch, low] if d < 2 else csend.at[s, ch]
-            recv = rrecv if d < 2 else crecv
+            if d < 2:
+                count = CH + 8 if isinstance(ch, int) and (s, ch) == (0, 0) else CH
+                source = rsend.at[s, ch, low, pl.ds(0, count)]
+                recv = rrecv.at[s, ch, low, pl.ds(0, count)]
+            else:
+                source, recv = csend.at[s, ch, low], crecv.at[s, ch, low]
             out.append(
                 pltpu.make_async_remote_copy(
-                    source, recv.at[s, ch, low], hs_sem.at[s, ch, d], hr_sem.at[s, ch, d],
+                    source, recv, hs_sem.at[s, ch, d], hr_sem.at[s, ch, d],
                     device_id=there, device_id_type=MESH,
                 )
             )
@@ -99,8 +122,8 @@
         moves = (
             (qb.at[CX - 8 : CX], qrow.at[0], near(1, 0)),
             (qb.at[0:8], qrow.at[1], near(-1, 0)),
-            (qb.at[:, 128:256], qcol.at[0], near(0, 1)),
-            (qb.at[:, 0:128], qcol.at[1], near(0, -1)),
+            (qcs.at[0], qcol.at[0], near(0, 1)),
+            (qcs.at[1], qcol.at[1], near(0, -1)),
         )
         return [
             pltpu.make_async_remote_copy(
@@ -111,28 +134,49 @@
 
     lane = lax.broadcasted_iota(jnp.int32, (8, 128), 1)
     lane3 = lax.broadcasted_iota(jnp.int32, (1, 8, 128), 2)
-    lane_col = lax.broadcasted_iota(jnp.int32, (CX, 128), 1)
+
+    def lanes_of(g):
+        return 32 * (g % 4), slice(8 * (g // 4), 8 * (g // 4) + 8)
+
+    def pack_pair(both, at, packed):
+        ends = pltpu.roll(jnp.where(lane < 64, both[:, :128], both[:, 128:]), at + 1, 1)
+        return jnp.where(lane == at, ends, packed[0]), jnp.where(lane == at + 1, ends, packed[1])
 
     def pack_edges(src, s, ch, extras=()):
-        for g in range(8):
-            packed = jnp.zeros((8, 128), F32)
-            for i in range(CH + len(extras)):
-                if i < CH:
-                    both = src[ch * CH + i, TAB + 8 * g : TAB + 8 * g + 8]
-                else:
-                    both = extras[i - CH][8 * g : 8 * g + 8]
-                ends = jnp.where(lane < 64, both[:, :128], both[:, 128:])
-                packed = jnp.where((lane >> 1) == i, pltpu.roll(ends, 2 * i + 1, 1), packed)
-            csend[s, ch, 8 * g : 8 * g + 8] = packed
+        for q in range(2):
+            packed = jnp.zeros((8, 128), F32), jnp.zeros((8, 128), F32)
+            for g in range(4 * q, 4 * q + 4):
+                base, part = lanes_of(g)
+                for i in range(CH + len(extras)):
+                    if i < CH:
+                        both = src[ch * CH + i, TAB + 8 * g : TAB + 8 * g + 8]
+                    else:
+                        both = extras[i - CH][8 * g : 8 * g + 8]
+                    packed = pack_pair(both, base + i, packed)
+            csend[s, ch, 0, part] = packed[0]
+            csend[s, ch, 1, part] = packed[1]
         for i in range(0, CH, 8):
             rsend[s, ch, 0, i : i + 8] = src[pl.ds(ch * CH + i, 8), TAB + CX - 1]
             rsend[s, ch, 1, i : i + 8] = src[pl.ds(ch * CH + i, 8), TAB]
+
+    def halo_send(s, ch):
         for copy in halo_copies(s, ch):
             copy.start()
 
+    def edge_send():
+        packed = jnp.zeros((8, 128), F32), jnp.zeros((8, 128), F32)
+        for g in range(8):
+            packed = pack_pair(qb[8 * g : 8 * g + 8], g, packed)
+        qcs[0], qcs[1] = packed
+        for copy in edge_copies():
+            copy.start()
+
+    def unpack_columns(s, ch):
+        ccomb[0] = crecv[s, ch, 0]
+        ccomb[1] = pltpu.roll(crecv[s, ch, 1], 126, 1)
+
     def unpack_edges(src, s, ch):
-        before, after = pltpu.roll(crecv[s, ch, 0], 1, 1), pltpu.roll(crecv[s, ch, 1], 127, 1)
-        ccomb[...] = jnp.where((lane_col & 1) == 1, before, after)
+        unpack_columns(s, ch)
         src[pl.ds(ch * CH, CH), TAB - 1] = rrecv[s, ch, 0, 0:CH]
         src[pl.ds(ch * CH, CH), TAB + CX] = rrecv[s, ch, 1, 0:CH]
 
@@ -152,11 +196,20 @@
         )
         return left, right
 
-    def ends_of(part, i, count):
-        columns = ccomb[part]
-        return jnp.concatenate(
-            [pltpu.roll(columns, lax.rem(255 - 2 * (i + j), 128), 1)[None] for j in range(count)], 0
-        )
+    def ends_of(g, i, count):
+        base, part = lanes_of(g)
+        low, high = ccomb[0, part], ccomb[1, part]
+        out = []
+        for j in range(count):
+            at = base + i + j
+            out.append(pltpu.roll(jnp.where(lane == at, low, high), lax.rem(128 - at, 128), 1)[None])
+        return jnp.concatenate(out, 0)
+
+    def put(dst, k, count, g, value):
+        if dst is out_state:
+            out_state[0, pl.ds(k, count), 8 * g : 8 * g + 8] = value
+        else:
+            dst[pl.ds(k, count), TAB + 8 * g : TAB + 8 * g + 8] = value
 
     def atm_batch(src, dst, k, count, ends, g):
         part, at = slice(8 * g, 8 * g + 8), TAB + 8 * g
@@ -171,13 +224,16 @@
         down = src[pl.ds(k, count), at + 1 : at + 9]
         left, right = sides(value, ends)
         new = c_own * value + c_mix * (before + after)
-        dst[pl.ds(k, count), at : at + 8] = (
-            new + (c_up * up + c_down * down) + (c_left * left + c_right * right)
-        )
+        new = new + (c_up * up + c_down * down) + (c_left * left + c_right * right)
+        put(dst, k, count, g, new)
 
     def cool(src, dst):
         rows = slice(TAB, TAB + CX)
-        dst[0, rows] = dst[0, rows] - coef[0, 2] * (src[0, rows] - forc[3])
+        heat = coef[0, 2] * (src[0, rows] - forc[3])
+        if dst is out_state:
+            dst[0, 0] = dst[0, 0] - heat
+        else:
+            dst[0, rows] = dst[0, rows] - heat
 
     def atm_chunk(src, dst, s, ch, wait=True):
         if wait:
@@ -186,7 +242,7 @@
 
         def batch(b, carry):
             for g in range(8):
-                ends = ends_of(slice(8 * g, 8 * g + 8), b * STACK, STACK)
+                ends = ends_of(g, b * STACK, STACK)
                 atm_batch(src, dst, ch * CH + b * STACK, STACK, ends, g)
             return carry
 
@@ -198,14 +254,19 @@
             pl.when(ch == 0)(lambda: cool(src, dst))
         if s < 2:
             pack_edges(dst, s + 1, ch)
+            halo_send(s + 1, ch)
 
     lane_all = lax.broadcasted_iota(jnp.int32, (CX, CY), 1)
 
     def around(plane, at):
         low_row = rrecv[0, 0, 0, CH + at : CH + at + 1]
         high_row = rrecv[0, 0, 1, CH + at : CH + at + 1]
-        low_col = crecv[0, 0, 0][:, 2 * (CH + at) : 2 * (CH + at) + 1]
-        high_col = crecv[0, 0, 1][:, 2 * (CH + at) + 1 : 2 * (CH + at) + 2]
+        low_col, high_col = [], []
+        for g in range(8):
+            base, part = lanes_of(g)
+            low_col.append(crecv[0, 0, 0, part][:, base + CH + at : base + CH + at + 1])
+            high_col.append(crecv[0, 0, 1, part][:, base + CH + at + 1 : base + CH + at + 2])
+        low_col, high_col = jnp.concatenate(low_col, 0), jnp.concatenate(high_col, 0)
         return (
             jnp.concatenate([low_row, plane[:-1]], 0),
             jnp.concatenate([plane[1:], high_row], 0),
@@ -224,30 +285,40 @@
         for at, other in enumerate(around(depth, 1)):
             cf[6 + at] = other
 
+    def first_halos():
+        for side, row in ((0, CX - 1), (1, 0)):
+            rsend[0, 0, side, CH : CH + 8] = jnp.zeros((8, CY), F32)
+            for at, plane in enumerate((kap, depth, c2)):
+                rsend[0, 0, side, CH + at : CH + at + 1] = plane[row : row + 1]
+        state_in(0).wait()
+        pack_edges(buf_a, 0, 0, (kap, depth, c2))
+
+    def other_halos():
+        def more(ch, carry):
+            state_in(ch).wait()
+            pack_edges(buf_a, 0, ch)
+            halo_send(0, ch)
+            return carry
+
+        lax.fori_loop(1, NCH, more, 0)
+
+    pl.when(is_atm)(first_halos)
+
+    def stage_links():
+        small_in[3].wait()
+        for n in range(9):
+            lnk_s[n] = remap[3:5, n * CAP : (n + 1) * CAP]
+
+    pl.when(is_ocn)(stage_links)
     pl.semaphore_wait(barrier, 24)
-    for side, row in ((0, CX - 1), (1, 0)):
-        rsend[0, 0, side, CH : CH + 8] = jnp.zeros((8, CY), F32)
-        for at, plane in enumerate((kap, depth, c2)):
-            rsend[0, 0, side, CH + at : CH + at + 1] = plane[row : row + 1]
-    state_in(0).wait()
-    pack_edges(buf_a, 0, 0, (kap, depth, c2))
-
-    def more(ch, carry):
-        state_in(ch).wait()
-        pack_edges(buf_a, 0, ch)
-        return carry
-
-    lax.fori_loop(1, NCH, more, 0)
-    for n in range(9):
-        lnk_s[n] = remap[3:5, n * CAP : (n + 1) * CAP]
-        if n != 4:
-            lnk_copy(n).start()
-    iota[...] = lax.broadcasted_iota(jnp.int32, (CY, 128), 0).astype(F32).astype(BF16)
 
     speed = 0.2 * jnp.sqrt(1.0 + forc[0] * forc[0] + forc[1] * forc[1])
 
     @pl.when(is_atm)
     def _():
+        halo_send(0, 0)
+        other_halos()
+        stage_links()
         halo_wait(0, 0)
         coefficients()
         atm_chunk(buf_a, buf_b, 0, 0, False)
@@ -255,20 +326,17 @@
         halo_wait(1, 0)
         unpack_edges(buf_b, 1, 0)
         for g in range(8):
-            part = slice(8 * g, 8 * g + 8)
-            atm_batch(buf_b, top, 0, 2, ends_of(part, 0, 2), g)
+            atm_batch(buf_b, top, 0, 2, ends_of(g, 0, 2), g)
         cool(buf_b, top)
         qb[...] = top[0, TAB : TAB + CX]
-        for copy in edge_copies():
-            copy.start()
+        edge_send()
         atm_chunk(buf_a, buf_b, 0, 2)
         for copy in edge_copies():
             copy.wait_recv()
         top[0, TAB - 1 : TAB] = qrow[0, 7:8]
         top[0, TAB + CX : TAB + CX + 1] = qrow[1, 0:1]
         for g in range(8):
-            part = slice(8 * g, 8 * g + 8)
-            ends = jnp.where(lane == 0, pltpu.roll(qcol[0, part], 1, 1), pltpu.roll(qcol[1, part], 127, 1))
+            ends = jnp.where(lane == 0, pltpu.roll(qcol[0], (128 - g) % 128, 1), pltpu.roll(qcol[1], 126 - g, 1))
             atm_batch(top, top2, 0, 1, ends[None], g)
         cool(top, top2)
         heat = c2 * (top2[0, TAB : TAB + CX] - forc[3])
@@ -279,6 +347,9 @@
 
     @pl.when(is_ocn)
     def _():
+        for n in range(9):
+            if n != 4:
+                lnk_copy(n).start()
         out_flux[0, 0] = speed * forc[0]
         out_flux[0, 1] = speed * forc[1]
 
@@ -312,14 +383,9 @@
     val_r[4] = val_s[4]
     acc[...] = jnp.zeros_like(acc)
 
-    def add(t, carry):
+    def add(t, arrived, fields):
         n = lax.rem(t + 4, 9)
-
-        @pl.when(n != 4)
-        def _():
-            lnk_copy(n).wait_recv()
-            val_copy(n).wait_recv()
-
+        pl.when(n != 4)(lambda: arrived(n))
         target = lnk_r[n, 0:1]
         weight = lnk_r[n, 1:2].astype(F32).astype(BF16)
         col = (target & (CY - 1)).astype(F32).astype(BF16)
@@ -330,17 +396,50 @@
         high0, low0 = hi_lo(val_r[n, 0:1])
         high1, low1 = hi_lo(val_r[n, 1:2])
         spread = jnp.concatenate(
-            [jnp.where(here, x, none) for x in (high0, high1, low0, low1, weight)], 0
-        )
-        acc[...] += lax.dot_general(
+            [jnp.where(here, x, none) for x in (high0, high1, low0, low1, weight)[:fields]], 0
+        )
+        acc[0 : fields * CX] += lax.dot_general(
             spread, hot, (((1,), (1,)), ((), ())), preferred_element_type=F32
         )
-        return carry
-
-    lax.fori_loop(0, 9, add, 0)
-    per = 1.0 / jnp.maximum(acc[4 * CX : 5 * CX], 1.0)
-    rem[0] = (acc[0:CX] + acc[2 * CX : 3 * CX]) * per
-    rem[1] = (acc[CX : 2 * CX] + acc[3 * CX : 4 * CX]) * per
+
+    per_copy = pltpu.make_async_remote_copy(
+        per.at[0], per.at[1], ps_sem, pr_sem, device_id=(1 - sec, tx, ty), device_id_type=MESH
+    )
+
+    @pl.when(is_atm)
+    def _():
+        def arrived(n):
+            lnk_pass(n).wait_recv()
+            val_copy(n).wait_recv()
+
+        def step(t, carry):
+            add(t, arrived, 4)
+            return carry
+
+        lax.fori_loop(0, 9, step, 0)
+        per_copy.wait_recv()
+
+    @pl.when(is_ocn)
+    def _():
+        first_halos()
+        halo_send(0, 0)
+        other_halos()
+        for n in range(9):
+            if n != 4:
+                lnk_copy(n).wait_recv()
+                lnk_pass(n).start()
+
+        def step(t, carry):
+            add(t, lambda n: val_copy(n).wait_recv(), 5)
+            return carry
+
+        lax.fori_loop(0, 9, step, 0)
+        per[0] = 1.0 / jnp.maximum(acc[4 * CX : 5 * CX], 1.0)
+        per_copy.start()
+        per[1] = per[0]
+
+    rem[0] = (acc[0:CX] + acc[2 * CX : 3 * CX]) * per[1]
+    rem[1] = (acc[CX : 2 * CX] + acc[3 * CX : 4 * CX]) * per[1]
 
     hand_over = pltpu.make_async_remote_copy(
         rem, hst, rs_sem, rr_sem, device_id=(1 - sec, tx, ty), device_id_type=MESH
@@ -363,13 +462,6 @@
         for g in range(1, 8):
             total = total + plane[8 * g : 8 * g + 8]
         return total[:, :128] + total[:, 128:]
-
-    def state_out(src, ch):
-        return pltpu.make_async_copy(
-            src.at[pl.ds(ch * CH, CH), pl.ds(TAB, CX)],
-            out_state.at[0, pl.ds(ch * CH, CH)],
-            out_sem.at[ch],
-        )
 
     @pl.when(is_atm)
     def _():
@@ -394,8 +486,7 @@
         lax.fori_loop(1, NCH, second, 0)
 
         def third(ch, carry):
-            atm_chunk(buf_a, buf_b, 2, ch)
-            state_out(buf_b, ch).start()
+            atm_chunk(buf_a, out_state, 2, ch)
             return carry
 
         lax.fori_loop(0, NCH, third, 0)
@@ -408,8 +499,6 @@
             for ch in range(NCH):
                 for copy in halo_copies(s, ch):
                     copy.wait_send()
-        for ch in range(NCH):
-            state_out(buf_b, ch).wait()
 
     @pl.when(is_ocn)
     def _():
@@ -419,6 +508,8 @@
         dec[...] = 0.5 * jnp.exp(level8 * (-1 / 8))
         halo_wait(0, 0)
         coefficients()
+
+        out_state[0, OLEV + STACK // 2 : LEV] = buf_a[OLEV + STACK // 2 : LEV, TAB : TAB + CX]
 
         def ocn_batch(src, dst, k, count, ends, g):
             part, at = slice(8 * g, 8 * g + 8), TAB + 8 * g
@@ -446,14 +537,14 @@
                 jnp.where(here + 1.0 < own, after - value, 0.0) + (before - value)
             )
             flow = flow - jnp.concatenate([fade, fade], 2) * (sx * (down - up) + sy * (right - left))
-            dst[pl.ds(k, count), at : at + 8] = value + jnp.where(here < own, flow, 0.0)
+            put(dst, k, count, g, value + jnp.where(here < own, flow, 0.0))
 
         def ocn_chunk(src, dst, s, ch):
             unpack_edges(src, s, ch)
 
             def batch(b, carry):
                 for g in range(8):
-                    ends = ends_of(slice(8 * g, 8 * g + 8), b * STACK, STACK)
+                    ends = ends_of(g, b * STACK, STACK)
                     ocn_batch(src, dst, ch * CH + b * STACK, STACK, ends, g)
                 return carry
 
@@ -467,31 +558,22 @@
 
             ocn_chunk(buf_a, buf_b, 0, ch)
             pack_edges(buf_b, 1, ch)
+            halo_send(1, ch)
             return carry
 
         lax.fori_loop(0, NCH, first, 0)
 
         def second(ch, carry):
             halo_wait(1, ch)
-            ocn_chunk(buf_b, buf_a, 1, ch)
-
-            @pl.when(ch > 0)
-            def _():
-                state_out(buf_a, ch).start()
-
+            ocn_chunk(buf_b, out_state, 1, ch)
             return carry
 
         lax.fori_loop(0, NCH, second, 0)
-        deep = pltpu.make_async_copy(
-            buf_a.at[pl.ds(2, CH - 2), pl.ds(TAB, CX)], out_state.at[0, pl.ds(2, CH - 2)], out_sem.at[0]
-        )
-        deep.start()
 
         gain = surface * 4.0 * c2
         hand_over.wait_recv()
         qb[...] = buf_b[0, TAB : TAB + CX] + gain * (hst[0] + 0.3 * hst[1])
-        for copy in edge_copies():
-            copy.start()
+        edge_send()
 
         total = jnp.zeros((16, 128), F32)
         for d in range(8):
@@ -514,68 +596,76 @@
             buf_b[0, at : at + 1] = qrow[side, inner : inner + 1] + fix * gain_of(
                 edge[CH + 2 : CH + 3], edge[CH + 1 : CH + 2]
             )
-        lane_c2, lane_depth = 2 * (CH + 2), 2 * (CH + 1)
-        low = gain_of(
-            pltpu.roll(crecv[0, 0, 0], 128 - lane_c2, 1), pltpu.roll(crecv[0, 0, 0], 128 - lane_depth, 1)
-        )
-        high = gain_of(
-            pltpu.roll(crecv[0, 0, 1], 126 - lane_c2, 1), pltpu.roll(crecv[0, 0, 1], 126 - lane_depth, 1)
-        )
-        surface_ends = jnp.where(
-            lane_col == 0,
-            pltpu.roll(qcol[0], 1, 1) + fix * low,
-            pltpu.roll(qcol[1], 127, 1) + fix * high,
-        )
-        unpack_columns = pltpu.roll(crecv[1, 0, 0], 1, 1), pltpu.roll(crecv[1, 0, 1], 127, 1)
-        ccomb[...] = jnp.where((lane_col & 1) == 1, unpack_columns[0], unpack_columns[1])
+        unpack_columns(1, 0)
         for g in range(8):
-            part = slice(8 * g, 8 * g + 8)
-            ends = jnp.concatenate([surface_ends[part][None], ends_of(part, 1, 1)], 0)
-            ocn_batch(buf_b, buf_a, 0, 2, ends, g)
-        buf_a[0, TAB : TAB + CX] = buf_a[0, TAB : TAB + CX] + gain * (flux0 + 0.3 * flux1)
-        shallow = pltpu.make_async_copy(
-            buf_a.at[pl.ds(0, 2), pl.ds(TAB, CX)], out_state.at[0, pl.ds(0, 2)], in_sem.at[0]
-        )
-        shallow.start()
+            base, part = lanes_of(g)
+            low, high = crecv[0, 0, 0, part], crecv[0, 0, 1, part]
+            at_depth, at_c2 = base + CH + 1, base + CH + 2
+            low = gain_of(pltpu.roll(low, 128 - at_c2, 1), pltpu.roll(low, 128 - at_depth, 1))
+            high = gain_of(pltpu.roll(high, 126 - at_c2, 1), pltpu.roll(high, 126 - at_depth, 1))
+            ends = jnp.where(
+                lane == 0,
+                pltpu.roll(qcol[0], (128 - g) % 128, 1) + fix * low,
+                pltpu.roll(qcol[1], 126 - g, 1) + fix * high,
+            )
+            ends = jnp.concatenate([ends[None], ends_of(g, 1, 1)], 0)
+            ocn_batch(buf_b, out_state, 0, 2, ends, g)
+        out_state[0, 0] = out_state[0, 0] + gain * (flux0 + 0.3 * flux1)
         for s in range(2):
             for ch in range(NCH):
                 for copy in halo_copies(s, ch):
                     copy.wait_send()
-        deep.wait()
-        for ch in range(1, NCH):
-            state_out(buf_a, ch).wait()
-        shallow.wait()
+        per_copy.wait_send()
+        for n in range(9):
+            if n != 4:
+                lnk_copy(n).wait_send()
+                lnk_pass(n).wait_send()
 
     for copy in edge_copies():
         copy.wait_send()
     for n in range(9):
         if n != 4:
-            lnk_copy(n).wait_send()
             val_copy(n).wait_send()
+
+
+def write_out(mid, flux, out_state, out_flux, sem):
+    copies = [
+        pltpu.make_async_copy(mid.at[:, pl.ds(12 * i, 12)], out_state.at[:, pl.ds(12 * i, 12)], sem.at[i])
+        for i in range(6)
+    ] + [pltpu.make_async_copy(flux, out_flux, sem.at[6])]
+    for copy in copies:
+        copy.start()
+    for copy in copies:
+        copy.wait()
 
 
 def on_device(state, coeffs, forcing, levels, remap):
     vmem = pl.BlockSpec(memory_space=pltpu.VMEM)
     anywhere = pl.BlockSpec(memory_space=pl.ANY)
+    hbm = pl.BlockSpec(memory_space=pltpu.HBM)
     dma = pltpu.SemaphoreType.DMA
-    return pl.pallas_call(
+    mid, flux = pl.pallas_call(
         kernel,
         out_shape=(
-            jax.ShapeDtypeStruct((1, LEV, CX, CY), F32),
-            jax.ShapeDtypeStruct((1, 4, CX, CY), F32),
+            pltpu.VMEM((1, LEV, CX, CY), F32),
+            pltpu.VMEM((1, 4, CX, CY), F32),
         ),
-        in_specs=[anywhere, vmem, vmem, vmem, vmem],
-        out_specs=(anywhere, vmem),
+        in_specs=[hbm] * 5,
+        out_specs=(vmem, vmem),
         scratch_shapes=[
+            pltpu.VMEM((1, 3, CX, CY), F32),
+            pltpu.VMEM((4, CX, CY), F32),
+            pltpu.VMEM((CX, CY), jnp.int32),
+            pltpu.VMEM((5, 9 * CAP), jnp.int32),
             pltpu.VMEM((LEV, CX + 16, CY), F32),
             pltpu.VMEM((LEV, CX + 16, CY), F32),
             pltpu.VMEM((2, CX + 16, CY), F32),
             pltpu.VMEM((2, CX + 16, CY), F32),
             pltpu.VMEM((3, NCH, 2, 32, CY), F32),
-            pltpu.VMEM((3, NCH, CX, 128), F32),
+            pltpu.VMEM((3, NCH, 2, 16, 128), F32),
             pltpu.VMEM((3, NCH, 2, 32, CY), F32),
-            pltpu.VMEM((3, NCH, 2, CX, 128), F32),
-            pltpu.VMEM((CX, 128), F32),
+            pltpu.VMEM((3, NCH, 2, 16, 128), F32),
+            pltpu.VMEM((2, 16, 128), F32),
             pltpu.VMEM((10, CX, CY), F32),
             pltpu.VMEM((9, 2, CAP), jnp.int32),
             pltpu.VMEM((9, 2, CAP), jnp.int32),
@@ -587,18 +677,23 @@
             pltpu.VMEM((LEV, 8, 128), F32),
             pltpu.VMEM((2, CX, CY), F32),
             pltpu.VMEM((2, CX, CY), F32),
+            pltpu.VMEM((2, CX, CY), F32),
             pltpu.VMEM((CX, CY), F32),
+            pltpu.VMEM((2, 8, 128), F32),
             pltpu.VMEM((2, 8, CY), F32),
-            pltpu.VMEM((2, CX, 128), F32),
+            pltpu.VMEM((2, 8, 128), F32),
             pltpu.VMEM((16, 128), F32),
             pltpu.VMEM((8, 16, 128), F32),
             pltpu.VMEM((8, 16, 128), F32),
-            dma((NCH,)),
-            dma((NCH,)),
+            dma((NCH + 4,)),
             dma((3, NCH, 4)),
             dma((3, NCH, 4)),
             dma((9,)),
             dma((9,)),
+            dma((9,)),
+            dma((9,)),
+            dma,
+            dma,
             dma((9,)),
             dma((9,)),
             dma,
@@ -611,10 +706,22 @@
             dma((8,)),
         ],
         compiler_params=pltpu.CompilerParams(
-            collective_id=0, has_side_effects=True, vmem_limit_bytes=60 << 20
+            collective_id=0, has_side_effects=True, vmem_limit_bytes=59 << 20
         ),
         name="window",
     )(state, coeffs, forcing, levels, remap)
+    return pl.pallas_call(
+        write_out,
+        out_shape=(
+            jax.ShapeDtypeStruct((1, LEV, CX, CY), F32),
+            jax.ShapeDtypeStruct((1, 4, CX, CY), F32),
+        ),
+        in_specs=[vmem, vmem],
+        out_specs=(anywhere, anywhere),
+        scratch_shapes=[dma((7,))],
+        compiler_params=pltpu.CompilerParams(vmem_limit_bytes=4 << 20),
+        name="write_out",
+    )(mid, flux)
 
 
 def solution(mesh):

time: 71.9 us -> 58.5 us (0.81)
  Pallas kernels: 65.1 us -> 57.6 us
  local copies, waits for them, and re-layouts: 5.85 us -> 0 us
    pallas_call x1 -> x2, Pallas kernels: 65.1 us -> 57.6 us  [the longest x1 55.3 us: on_device(): pl.pallas_call(kernel, out_shape=(pltpu.VMEM((1, LEV, CX, CY), F32), pltp...]
    unnamed x4 -> x0, local copies, waits for them, and re-layouts: 5.85 us -> none
where the time goes in v3:
time: 58.5 us; the launch traced here: 58.4 us
  Pallas kernels  57.6 us (98%)
  between operations  0.8 us (1%)
    pallas_call x1, Pallas kernels, on_device(): pl.pallas_call(kernel, out_shape=(pltpu.VMEM((1, LEV, CX, CY), F32), pltp...  55.3 us
    pallas_call x1, Pallas kernels, on_device(): pl.pallas_call(write_out, out_shape=(jax.ShapeDtypeStruct((1, LEV, CX, CY...  2.32 us

profile of v3, /device:TPU:0, one launch (start us, length us, event | category | flops | bytes accessed | tf_op | source)
XLA Modules:
  0.0 58.4 jit_solution(18298611448117091857)
XLA Ops:
  0.6 55.3 %window.1 = (f32[1,72,64,256]{3,2,1,0:T(8,128)S(1)}, f32[1,4,64,256]{3,2,1,0:T(8,128)S(1)}) custom-call(f32[1,72,64,256]{3,2,1,0:T(8,128)} %state.1, f32[1,3,64,256]{3,2,1,0:T(8,128)} %coef_in.1, f32[4,64,256]{2,1,0:T(8,128)} %forc_in.1, s32[64,256]{1,0:T(8,128)} %lev_in.1, s32[5,36864]{1,0:T(8,128)} %remap_in.1), custom_call_target="tpu_custom_call" | custom-call | tf_op jit(solution)/shard_map/window/pallas_call | solution.py:647
  55.9 2.3 %write_out.1 = (f32[1,72,64,256]{3,2,1,0:T(8,128)}, f32[1,4,64,256]{3,2,1,0:T(8,128)}) custom-call(f32[1,72,64,256]{3,2,1,0:T(8,128)S(1)} %get-tuple-element.4.mid, f32[1,4,64,256]{3,2,1,0:T(8,128)S(1)} %get-tuple-element.5.flux), custom_call_target="tpu_custom_call" | custom-call | tf_op jit(solution)/shard_map/write_out/pallas_call | solution.py:713

commit v4 on v3

--- a/solution.py
+++ b/solution.py
@@ -10,7 +10,7 @@
 TAB = 8
 CH = 24
 NCH = LEV // CH
-STACK = 8
+STACK = 6
 F32, BF16 = jnp.float32, jnp.bfloat16
 MESH = pl.DeviceIdType.MESH
 
@@ -45,10 +45,9 @@
                 pl.semaphore_signal(barrier, 1, device_id=near(dx, dy), device_id_type=MESH)
     for dy in range(2, 7):
         pl.semaphore_signal(barrier, 1, device_id=near(0, dy), device_id_type=MESH)
-    for dx in range(8):
-        pl.semaphore_signal(
-            barrier, 1, device_id=(1 - sec, lax.rem(tx + dx, 8), ty), device_id_type=MESH
-        )
+    for dx in (2, 3, 5, 6):
+        pl.semaphore_signal(barrier, 1, device_id=near(dx, 0), device_id_type=MESH)
+    pl.semaphore_signal(barrier, 1, device_id=(1 - sec, tx, ty), device_id_type=MESH)
 
     def state_in(ch):
         return pltpu.make_async_copy(
@@ -310,7 +309,7 @@
             lnk_s[n] = remap[3:5, n * CAP : (n + 1) * CAP]
 
     pl.when(is_ocn)(stage_links)
-    pl.semaphore_wait(barrier, 24)
+    pl.semaphore_wait(barrier, 21)
 
     speed = 0.2 * jnp.sqrt(1.0 + forc[0] * forc[0] + forc[1] * forc[1])
 
@@ -331,6 +330,7 @@
         qb[...] = top[0, TAB : TAB + CX]
         edge_send()
         atm_chunk(buf_a, buf_b, 0, 2)
+        atm_chunk(buf_b, buf_a, 1, 0, False)
         for copy in edge_copies():
             copy.wait_recv()
         top[0, TAB - 1 : TAB] = qrow[0, 7:8]
@@ -347,9 +347,6 @@
 
     @pl.when(is_ocn)
     def _():
-        for n in range(9):
-            if n != 4:
-                lnk_copy(n).start()
         out_flux[0, 0] = speed * forc[0]
         out_flux[0, 1] = speed * forc[1]
 
@@ -375,6 +372,10 @@
         @pl.when(n != 4)
         def _():
             val_copy(n).start()
+
+        @pl.when(jnp.logical_and(is_ocn, n != 4))
+        def _():
+            lnk_copy(n).start()
 
         return carry
 
@@ -438,8 +439,8 @@
         per_copy.start()
         per[1] = per[0]
 
-    rem[0] = (acc[0:CX] + acc[2 * CX : 3 * CX]) * per[1]
-    rem[1] = (acc[CX : 2 * CX] + acc[3 * CX : 4 * CX]) * per[1]
+    rem[0:CX] = (acc[0:CX] + acc[2 * CX : 3 * CX]) * per[1]
+    rem[CX : 2 * CX] = (acc[CX : 2 * CX] + acc[3 * CX : 4 * CX]) * per[1]
 
     hand_over = pltpu.make_async_remote_copy(
         rem, hst, rs_sem, rr_sem, device_id=(1 - sec, tx, ty), device_id_type=MESH
@@ -454,30 +455,19 @@
     def along_tx(d):
         return pltpu.make_async_remote_copy(
             red1.at[0], red2.at[d], p2s_sem.at[d], p2r_sem.at[d],
-            device_id=(1 - sec, lax.rem(tx + d, 8), ty), device_id_type=MESH,
+            device_id=near(d, 0), device_id_type=MESH,
         )
 
     def folded(plane):
         total = plane[0:8]
         for g in range(1, 8):
             total = total + plane[8 * g : 8 * g + 8]
-        return total[:, :128] + total[:, 128:]
+        return total
 
     @pl.when(is_atm)
     def _():
+        rem[2 * CX : 2 * CX + 8] = folded(out_flux[0, 0])
         hand_over.start()
-        red[0:8] = folded(out_flux[0, 0] - surface * rem[0])
-        red[8:16] = folded(surface)
-        for d in range(1, 8):
-            along_ty(d).start()
-        atm_chunk(buf_b, buf_a, 1, 0, False)
-        total = red[...]
-        for d in range(1, 8):
-            along_ty(d).wait_recv()
-            total = total + red1[d]
-        red1[0] = total
-        for d in range(8):
-            along_tx(d).start()
 
         def second(ch, carry):
             atm_chunk(buf_b, buf_a, 1, ch)
@@ -490,10 +480,6 @@
             return carry
 
         lax.fori_loop(0, NCH, third, 0)
-        for d in range(1, 8):
-            along_ty(d).wait_send()
-        for d in range(8):
-            along_tx(d).wait_send()
         hand_over.wait_send()
         for s in range(3):
             for ch in range(NCH):
@@ -502,22 +488,24 @@
 
     @pl.when(is_ocn)
     def _():
-        out_flux[0, 2] = surface * rem[0]
-        out_flux[0, 3] = surface * rem[1]
+        out_flux[0, 2] = surface * rem[0:CX]
+        out_flux[0, 3] = surface * rem[CX : 2 * CX]
         level8 = lax.broadcasted_iota(jnp.int32, (LEV, 8, 128), 0).astype(F32)
         dec[...] = 0.5 * jnp.exp(level8 * (-1 / 8))
         halo_wait(0, 0)
         coefficients()
 
-        out_state[0, OLEV + STACK // 2 : LEV] = buf_a[OLEV + STACK // 2 : LEV, TAB : TAB + CX]
+        out_state[0, OLEV:LEV] = buf_a[OLEV:LEV, TAB : TAB + CX]
 
         def ocn_batch(src, dst, k, count, ends, g):
             part, at = slice(8 * g, 8 * g + 8), TAB + 8 * g
-            c_up, c_down, c_left, c_right, c_mix = [cf[i, part][None] for i in range(5)]
+            c_up, c_down, c_left, c_right, c_mix, c_own = [cf[i, part][None] for i in range(6)]
             d_up, d_down, d_left, d_right = [cf[i, part][None] for i in range(6, 10)]
             own = lev[part].astype(F32)[None]
             sx, sy = out_flux[0, 2, part][None], out_flux[0, 3, part][None]
-            here = (lax.broadcasted_iota(jnp.int32, (count, 8, CY), 0) + k).astype(F32)
+            here = jnp.concatenate(
+                [jnp.full((1, 8, CY), jnp.asarray(k + i, jnp.int32).astype(F32), F32) for i in range(count)], 0
+            )
             fade = dec[pl.ds(k, count)]
             value = src[pl.ds(k, count), at : at + 8]
             before = src[pl.ds(jnp.maximum(k - 1, 0), 1), at : at + 8]
@@ -527,17 +515,16 @@
             up = src[pl.ds(k, count), at - 1 : at + 7]
             down = src[pl.ds(k, count), at + 1 : at + 9]
             left, right = sides(value, ends)
-            flow = (
-                jnp.where(here < d_up, c_up * (up - value), 0.0)
-                + jnp.where(here < d_down, c_down * (down - value), 0.0)
-                + jnp.where(here < d_left, c_left * (left - value), 0.0)
-                + jnp.where(here < d_right, c_right * (right - value), 0.0)
+            new = c_own * value + c_mix * (jnp.where(here + 1.0 < own, after, value) + before)
+            new = new + (
+                c_up * jnp.where(here < d_up, up, value) + c_down * jnp.where(here < d_down, down, value)
             )
-            flow = flow + c_mix * (
-                jnp.where(here + 1.0 < own, after - value, 0.0) + (before - value)
+            new = new + (
+                c_left * jnp.where(here < d_left, left, value)
+                + c_right * jnp.where(here < d_right, right, value)
             )
-            flow = flow - jnp.concatenate([fade, fade], 2) * (sx * (down - up) + sy * (right - left))
-            put(dst, k, count, g, value + jnp.where(here < own, flow, 0.0))
+            new = new - jnp.concatenate([fade, fade], 2) * (sx * (down - up) + sy * (right - left))
+            put(dst, k, count, g, jnp.where(here < own, new, value))
 
         def ocn_chunk(src, dst, s, ch):
             unpack_edges(src, s, ch)
@@ -548,7 +535,7 @@
                     ocn_batch(src, dst, ch * CH + b * STACK, STACK, ends, g)
                 return carry
 
-            batches = jnp.minimum(CH, OLEV - ch * CH + STACK - 1) // STACK
+            batches = jnp.minimum(CH, OLEV - ch * CH) // STACK
             lax.fori_loop(0, batches, batch, 0)
 
         def first(ch, carry):
@@ -563,25 +550,36 @@
 
         lax.fori_loop(0, NCH, first, 0)
 
-        def second(ch, carry):
+        def second(ch):
             halo_wait(1, ch)
             ocn_chunk(buf_b, out_state, 1, ch)
-            return carry
-
-        lax.fori_loop(0, NCH, second, 0)
+
+        second(0)
 
         gain = surface * 4.0 * c2
         hand_over.wait_recv()
-        qb[...] = buf_b[0, TAB : TAB + CX] + gain * (hst[0] + 0.3 * hst[1])
+        heat_in, fresh_in = hst[0:CX], hst[CX : 2 * CX]
+        for i, plane in enumerate((hst[2 * CX : 2 * CX + 8] - folded(surface * heat_in), folded(surface))):
+            red[8 * i : 8 * i + 8] = plane[:, :128] + plane[:, 128:]
+        for d in range(1, 8):
+            along_ty(d).start()
+        qb[...] = buf_b[0, TAB : TAB + CX] + gain * (heat_in + 0.3 * fresh_in)
         edge_send()
-
-        total = jnp.zeros((16, 128), F32)
-        for d in range(8):
+        second(1)
+        total = red[...]
+        for d in range(1, 8):
+            along_ty(d).wait_recv()
+            total = total + red1[d]
+        red1[0] = total
+        for d in range(1, 8):
+            along_tx(d).start()
+        second(2)
+        for d in range(1, 8):
             along_tx(d).wait_recv()
             total = total + red2[d]
         fix = jnp.sum(total[0:8], keepdims=True) / jnp.maximum(jnp.sum(total[8:16], keepdims=True), 1.0)
-        flux0 = surface * (hst[0] + fix)
-        flux1 = surface * hst[1]
+        flux0 = surface * (heat_in + fix)
+        flux1 = surface * fresh_in
         out_flux[0, 0] = flux0
         out_flux[0, 1] = flux1
         buf_b[0, TAB : TAB + CX] = qb[...] + gain * fix
@@ -615,6 +613,9 @@
             for ch in range(NCH):
                 for copy in halo_copies(s, ch):
                     copy.wait_send()
+        for d in range(1, 8):
+            along_ty(d).wait_send()
+            along_tx(d).wait_send()
         per_copy.wait_send()
         for n in range(9):
             if n != 4:
@@ -675,8 +676,8 @@
             pltpu.VMEM((4 * CX, CY), BF16),
             pltpu.VMEM((CY, 128), BF16),
             pltpu.VMEM((LEV, 8, 128), F32),
-            pltpu.VMEM((2, CX, CY), F32),
-            pltpu.VMEM((2, CX, CY), F32),
+            pltpu.VMEM((2 * CX + 8, CY), F32),
+            pltpu.VMEM((2 * CX + 8, CY), F32),
             pltpu.VMEM((2, CX, CY), F32),
             pltpu.VMEM((CX, CY), F32),
             pltpu.VMEM((2, 8, 128), F32),

time: 58.5 us -> 53.9 us (0.921)
  Pallas kernels: 57.6 us -> 52.9 us
    pallas_call x1, Pallas kernels: 55.3 us -> 50.6 us  [on_device(): pl.pallas_call(kernel, out_shape=(pltpu.VMEM((1, LEV, CX, CY), F32), pltp...]
where the time goes in v4:
time: 53.9 us; the launch traced here: 53.7 us
  Pallas kernels  52.9 us (98%)
  between operations  0.8 us (1%)
    pallas_call x1, Pallas kernels, on_device(): pl.pallas_call(kernel, out_shape=(pltpu.VMEM((1, LEV, CX, CY), F32), pltp...  50.6 us
    pallas_call x1, Pallas kernels, on_device(): pl.pallas_call(write_out, out_shape=(jax.ShapeDtypeStruct((1, LEV, CX, CY...  2.32 us

profile of v4, /device:TPU:0, one launch (start us, length us, event | category | flops | bytes accessed | tf_op | source)
XLA Modules:
  0.0 53.7 jit_solution(4878570338692673721)
XLA Ops:
  0.6 50.6 %window.1 = (f32[1,72,64,256]{3,2,1,0:T(8,128)S(1)}, f32[1,4,64,256]{3,2,1,0:T(8,128)S(1)}) custom-call(f32[1,72,64,256]{3,2,1,0:T(8,128)} %state.1, f32[1,3,64,256]{3,2,1,0:T(8,128)} %coef_in.1, f32[4,64,256]{2,1,0:T(8,128)} %forc_in.1, s32[64,256]{1,0:T(8,128)} %lev_in.1, s32[5,36864]{1,0:T(8,128)} %remap_in.1), custom_call_target="tpu_custom_call" | custom-call | tf_op jit(solution)/shard_map/window/pallas_call | solution.py:648
  51.3 2.3 %write_out.1 = (f32[1,72,64,256]{3,2,1,0:T(8,128)}, f32[1,4,64,256]{3,2,1,0:T(8,128)}) custom-call(f32[1,72,64,256]{3,2,1,0:T(8,128)S(1)} %get-tuple-element.4.mid, f32[1,4,64,256]{3,2,1,0:T(8,128)S(1)} %get-tuple-element.5.flux), custom_call_target="tpu_custom_call" | custom-call | tf_op jit(solution)/shard_map/write_out/pallas_call | solution.py:714

commit v5 on v4

--- a/solution.py
+++ b/solution.py
@@ -234,7 +234,7 @@
         else:
             dst[0, rows] = dst[0, rows] - heat
 
-    def atm_chunk(src, dst, s, ch, wait=True):
+    def atm_chunk(src, dst, s, ch, wait=True, STACK=12):
         if wait:
             halo_wait(s, ch)
         unpack_edges(src, s, ch)
@@ -357,45 +357,54 @@
     one, none = jnp.array(1, BF16), jnp.array(0, BF16)
 
     def pick(t, carry):
-        n = lax.rem(t + 5, 9)
-        at = pl.multiple_of(n * CAP, CAP)
-        source = remap[0:1, pl.ds(at, CAP)]
-        weight = remap[4:5, pl.ds(at, CAP)].astype(F32)
+        m = lax.rem(t + 2, 3)
+        at = pl.multiple_of(m * 3 * CAP, 3 * CAP)
+        source = remap[0:1, pl.ds(at, 3 * CAP)]
+        weight = remap[4:5, pl.ds(at, 3 * CAP)].astype(F32)
         col = (source & (CY - 1)).astype(F32).astype(BF16)
-        hot = jnp.where(wide(iota[...], CAP // 128) == col, one, none)
+        hot = jnp.where(wide(iota[...], 3 * CAP // 128) == col, one, none)
         product = jnp.dot(fb[...], hot, preferred_element_type=F32)
-        here = lax.broadcasted_iota(jnp.int32, (CX, CAP), 0) == (source >> 8)
+        here = lax.broadcasted_iota(jnp.int32, (CX, 3 * CAP), 0) == (source >> 8)
         for c in range(2):
             both = product[CX * c : CX * (c + 1)] + product[2 * CX + CX * c : 2 * CX + CX * (c + 1)]
-            val_s[n, c : c + 1] = jnp.sum(jnp.where(here, both, 0.0), 0, keepdims=True) * weight
-
-        @pl.when(n != 4)
-        def _():
-            val_copy(n).start()
-
-        @pl.when(jnp.logical_and(is_ocn, n != 4))
-        def _():
-            lnk_copy(n).start()
+            picked = jnp.sum(jnp.where(here, both, 0.0), 0, keepdims=True) * weight
+            for j in range(3):
+                val_s[3 * m + j, c : c + 1] = picked[:, j * CAP : (j + 1) * CAP]
+        for j in range(3):
+            n = 3 * m + j
+
+            @pl.when(n != 4)
+            def _(n=n):
+                val_copy(n).start()
+
+            @pl.when(jnp.logical_and(is_ocn, n != 4))
+            def _(n=n):
+                lnk_copy(n).start()
 
         return carry
 
-    lax.fori_loop(0, 9, pick, 0)
+    lax.fori_loop(0, 3, pick, 0)
     lnk_r[4] = lnk_s[4]
     val_r[4] = val_s[4]
     acc[...] = jnp.zeros_like(acc)
 
     def add(t, arrived, fields):
-        n = lax.rem(t + 4, 9)
-        pl.when(n != 4)(lambda: arrived(n))
-        target = lnk_r[n, 0:1]
-        weight = lnk_r[n, 1:2].astype(F32).astype(BF16)
+        m = lax.rem(t + 2, 3)
+        for j in range(3):
+            pl.when(3 * m + j != 4)(lambda j=j: arrived(3 * m + j))
+
+        def three(ref, row):
+            return jnp.concatenate([ref[3 * m + j, row : row + 1] for j in range(3)], 1)
+
+        target = three(lnk_r, 0)
+        weight = three(lnk_r, 1).astype(F32).astype(BF16)
         col = (target & (CY - 1)).astype(F32).astype(BF16)
         row = (target >> 8).astype(F32).astype(BF16)
-        index = wide(iota[...], CAP // 128)
+        index = wide(iota[...], 3 * CAP // 128)
         hot = jnp.where(index == col, one, none)
         here = index[:CX] == row
-        high0, low0 = hi_lo(val_r[n, 0:1])
-        high1, low1 = hi_lo(val_r[n, 1:2])
+        high0, low0 = hi_lo(three(val_r, 0))
+        high1, low1 = hi_lo(three(val_r, 1))
         spread = jnp.concatenate(
             [jnp.where(here, x, none) for x in (high0, high1, low0, low1, weight)[:fields]], 0
         )
@@ -417,7 +426,7 @@
             add(t, arrived, 4)
             return carry
 
-        lax.fori_loop(0, 9, step, 0)
+        lax.fori_loop(0, 3, step, 0)
         per_copy.wait_recv()
 
     @pl.when(is_ocn)
@@ -434,7 +443,7 @@
             add(t, lambda n: val_copy(n).wait_recv(), 5)
             return carry
 
-        lax.fori_loop(0, 9, step, 0)
+        lax.fori_loop(0, 3, step, 0)
         per[0] = 1.0 / jnp.maximum(acc[4 * CX : 5 * CX], 1.0)
         per_copy.start()
         per[1] = per[0]

time: 53.9 us -> 52.8 us (0.980)
  Pallas kernels: 52.9 us -> 51.4 us
    pallas_call x1, Pallas kernels: 50.6 us -> 49.1 us  [on_device(): pl.pallas_call(kernel, out_shape=(pltpu.VMEM((1, LEV, CX, CY), F32), pltp...]
where the time goes in v5:
time: 52.8 us; the launch traced here: 52.2 us
  Pallas kernels  51.4 us (97%)
  between operations  0.8 us (2%)
    pallas_call x1, Pallas kernels, on_device(): pl.pallas_call(kernel, out_shape=(pltpu.VMEM((1, LEV, CX, CY), F32), pltp...  49.1 us
    pallas_call x1, Pallas kernels, on_device(): pl.pallas_call(write_out, out_shape=(jax.ShapeDtypeStruct((1, LEV, CX, CY...  2.32 us

profile of v5, /device:TPU:0, one launch (start us, length us, event | category | flops | bytes accessed | tf_op | source)
XLA Modules:
  0.0 52.2 jit_solution(15827694570293424384)
XLA Ops:
  0.6 49.1 %window.1 = (f32[1,72,64,256]{3,2,1,0:T(8,128)S(1)}, f32[1,4,64,256]{3,2,1,0:T(8,128)S(1)}) custom-call(f32[1,72,64,256]{3,2,1,0:T(8,128)} %state.1, f32[1,3,64,256]{3,2,1,0:T(8,128)} %coef_in.1, f32[4,64,256]{2,1,0:T(8,128)} %forc_in.1, s32[64,256]{1,0:T(8,128)} %lev_in.1, s32[5,36864]{1,0:T(8,128)} %remap_in.1), custom_call_target="tpu_custom_call" | custom-call | tf_op jit(solution)/shard_map/window/pallas_call | solution.py:657
  49.7 2.3 %write_out.1 = (f32[1,72,64,256]{3,2,1,0:T(8,128)}, f32[1,4,64,256]{3,2,1,0:T(8,128)}) custom-call(f32[1,72,64,256]{3,2,1,0:T(8,128)S(1)} %get-tuple-element.4.mid, f32[1,4,64,256]{3,2,1,0:T(8,128)S(1)} %get-tuple-element.5.flux), custom_call_target="tpu_custom_call" | custom-call | tf_op jit(solution)/shard_map/write_out/pallas_call | solution.py:723
